TPU v7x, 128 devices: a whole 4x4x4 slice. The times are simulated.
128 devices in a mesh: lat: 64 (over z, y, x), lon: 2 (over core).
Axes of the slice: x: 4, y: 4, z: 4, core: 2. Of those that a mesh axis runs over, the one named last changes fastest.
Arguments:
- grid_field: bfloat16 [384, 1440, 512], P('lat', 'lon'), may hold values from -6 to 6
- basis_values: bfloat16 [384, 24, 4], P('lat'), may hold values from -3 to 3
- support_lat: int32 [384, 24], P('lat'), may hold values from -1 to 1
- support_lon: int32 [384, 24], P('lat'), may hold values from -12 to 12
- lon_reach: int32 [384], P('lat'), may hold values from 1 to 12, as said below
- mix_weights: bfloat16 [4, 512, 512], replicated, may hold values from -0.125 to 0.125
Outputs:
- spectra: bfloat16 [2, 640, 384, 512], P(None, 'lat', None, 'lon')
Inputs may be any that keep to these rules, and one draw needn't show every extreme that they name: `lon_reach`: roughly larger toward the window's first and last rows, and equal to 12 in both of those rows.
All inputs are finite; a program needn't handle non-finite values.
Results may differ from a plain program's by a relative error of at most 0.0063.
Values may be sent and summed in bfloat16 or wider, within the bound.
No kernel may reach another device: no remote copies, remote signals or barrier semaphores. Data moves between devices by JAX's collectives and lax.ppermute only.
A program may use at most 192 MiB of HBM per device.

v0:
```python
import jax
import jax.numpy as jnp
from jax import lax
from jax.sharding import PartitionSpec as P

MMAX = 640
K = 4
RLAT = 1
HMAX = 12


def extended_2(block, sides, width, periodic):
    for axis, dim in sides:
        count = lax.axis_size(axis)
        forward = [(i, i + 1) for i in range(count - 1)]
        if periodic:
            forward.append((count - 1, 0))
        backward = [(target, source) for source, target in forward]
        low = lax.ppermute(
            lax.slice_in_dim(block, block.shape[dim] - width, None, axis=dim), axis, forward
        )
        high = lax.ppermute(lax.slice_in_dim(block, 0, width, axis=dim), axis, backward)
        block = jnp.concatenate([low, block, high], axis=dim)
    return block


def dft_table(length_lon, mode_count):
    col_ids = jnp.arange(length_lon, dtype=jnp.int32)
    mode_ids = jnp.arange(mode_count, dtype=jnp.int32)
    product = col_ids[:, None] * mode_ids[None, :] % length_lon
    angles = product.astype(jnp.float32) * (2.0 * jnp.pi / length_lon)
    factor = 1.0 / jnp.sqrt(jnp.float32(length_lon))
    return jnp.stack([jnp.cos(angles) * factor, -jnp.sin(angles) * factor], axis=1).astype(
        jnp.bfloat16
    )


def aggregate_block(extended, col_start, lon_cols, support_lat, lon_shift, basis_values):
    lat_rows = support_lat.shape[0]
    support_count = support_lat.shape[1]
    channels = extended.shape[2]
    span_lat = 2 * RLAT + 1
    width = lon_cols + 2 * HMAX
    block_size = min(8, support_count)
    col_ids = jnp.arange(lon_cols, dtype=jnp.int32)

    def one_row(row_item):
        row_index, lat_step, lon_step, basis_row = row_item
        window = lax.dynamic_slice(
            extended, (row_index, col_start - HMAX, jnp.int32(0)), (span_lat, width, channels)
        )
        flat_window = window.reshape(span_lat * width, channels)
        flat_index = (
            (lat_step[:, None] + RLAT) * width + HMAX + lon_step[:, None] + col_ids[None, :]
        )
        total = jnp.zeros((lon_cols, K, channels), jnp.float32)
        for first in range(0, support_count, block_size):
            last = min(first + block_size, support_count)
            picked = jnp.take(flat_window, flat_index[first:last], axis=0)
            total = total + jnp.einsum(
                "sjc,sk->jkc", picked, basis_row[first:last], preferred_element_type=jnp.float32
            )
        return total.astype(jnp.bfloat16)

    return lax.map(
        one_row, (jnp.arange(lat_rows, dtype=jnp.int32), support_lat, lon_shift, basis_values)
    )


def body(grid_field, basis_values, support_lat, support_lon, lon_reach, mix_weights):
    lat_rows, lon_cols, channels = grid_field.shape
    lon_groups = lax.axis_size("lon")
    total_lon = lon_cols * lon_groups
    with_rows = extended_2(grid_field, (("lat", 0),), RLAT, False)
    lon_shift = jnp.clip(support_lon, -lon_reach[:, None], lon_reach[:, None])
    twiddle = dft_table(total_lon, MMAX)
    extended = extended_2(with_rows, (("lon", 1),), HMAX, True)
    aggregated = aggregate_block(
        extended, jnp.int32(HMAX), lon_cols, support_lat, lon_shift, basis_values
    )
    convolved = jnp.dot(
        aggregated.reshape(lat_rows * lon_cols, K * channels),
        mix_weights.reshape(K * channels, channels),
        preferred_element_type=jnp.float32,
    )
    activated = (
        jax.nn.gelu(convolved, approximate=False)
        .astype(jnp.bfloat16)
        .reshape(lat_rows, lon_cols, channels)
    )
    zonal = jnp.einsum(
        "ljc,jtm->tmlc",
        lax.all_to_all(activated, "lon", split_axis=2, concat_axis=1, tiled=True),
        twiddle,
        preferred_element_type=jnp.float32,
    ).astype(jnp.bfloat16)
    return lax.all_to_all(zonal, "lat", split_axis=1, concat_axis=2, tiled=True)


def solution(mesh):
    return jax.shard_map(
        body,
        mesh=mesh,
        in_specs=(
            P("lat", "lon", None),
            P("lat", None, None),
            P("lat", None),
            P("lat", None),
            P("lat"),
            P(),
        ),
        out_specs=P(None, "lat", None, "lon"),
        check_vma=False,
    )
```

profile of v0, /device:TPU:1, one launch (start us, length us, event | category | flops | bytes accessed | tf_op | source)
XLA Modules:
  0.0 826.6 jit_solution(13651768506153008866)
XLA Ops:
  7.8 17.0 %multiply_convert_fusion = (bf16[1440,1,640]{2,0,1:T(8,128)(2,1)}, bf16[1440,1,640]{2,0,1:T(8,128)(2,1)}) fusion(), kind=kLoop, calls=%fused_computation.73 | loop fusion | flops 12902400 | bytes 3686400 | tf_op jit(solution)/shard_map/convert.1
  39.3 625.6 %while.11 = (s32[]{:T(128)}, bf16[6,720,4,512]{3,2,1,0:T(4,128)(2,1)}, bf16[6,24,4]{1,2,0:T(4,128)(2,1)}, s32[6]{0:T(128)S(1)}, bf16[8,744,512]{2,1,0:T(8,128)(2...) while((s32[]{:T(128)}, ...), condition=%wide.region_1.3_spmd.clone, body=%wide.region_0.2_spmd.clone.sunk | while | flops 84241248 | bytes 84895200 | solution.py:65
  57.3 19.5 %gather_fusion.1 = bf16[5760,512]{1,0:T(8,128)(2,1)} fusion(bf16[2232,512]{1,0:T(8,128)(2,1)} %bitcast.71, s32[6144]{0:T(1024)S(1)} %pad_clamp_fusion.7), kind=kCustom, calls=%fused_computation.1.clone.clone.1 | custom fusion | bytes 11819520 | tf_op jit(solution)/shard_map/while/body/eval_jaxpr/jit(_take)/gather | solution.py:59
  77.8 11.5 %fusion.63 = f32[4,720,512]{2,0,1:T(4,128)} fusion(bf16[8,720,512]{2,1,0:T(8,128)(2,1)} %bitcast.74, pred[8,720]{0,1:T(8,128)(4,1)S(1)} %copy.65, bf16[1,24,4]{1,2,0:T(4,128)(2,1)S(1)} %constant_dynamic-slice_fusion.7), kind=kOutput, calls=%fused_computation.7.clone.1 | convolution fusion | flops 26542080 | bytes 11802432 | tf_op jit(solution)/shard_map/while/body/eval_jaxpr/sjc,sk->jkc/dot_general | solution.py:60
  89.4 19.5 %gather_fusion = bf16[5760,512]{1,0:T(8,128)(2,1)} fusion(bf16[2232,512]{1,0:T(8,128)(2,1)} %bitcast.72, s32[6144]{0:T(1024)S(1)} %pad_clamp_fusion.6), kind=kCustom, calls=%fused_computation.2.clone.clone.1 | custom fusion | bytes 11819520 | tf_op jit(solution)/shard_map/while/body/eval_jaxpr/jit(_take)/gather | solution.py:59
  109.1 11.5 %fusion.62 = f32[4,720,512]{2,0,1:T(4,128)} fusion(bf16[8,720,512]{2,1,0:T(8,128)(2,1)} %bitcast.76, pred[8,720]{0,1:T(8,128)(4,1)S(1)} %copy.64, bf16[1,24,4]{1,2,0:T(4,128)(2,1)S(1)} %constant_dynamic-slice_fusion.7), kind=kOutput, calls=%fused_computation.5.clone.1 | convolution fusion | flops 26542080 | bytes 11802432 | tf_op jit(solution)/shard_map/while/body/eval_jaxpr/sjc,sk->jkc/dot_general | solution.py:60
  120.7 19.5 %gather_fusion.2 = bf16[5760,512]{1,0:T(8,128)(2,1)} fusion(bf16[2232,512]{1,0:T(8,128)(2,1)} %bitcast.73, s32[6144]{0:T(1024)S(1)} %pad_clamp_fusion.8), kind=kCustom, calls=%fused_computation.clone.clone.1 | custom fusion | bytes 11819520 | tf_op jit(solution)/shard_map/while/body/eval_jaxpr/jit(_take)/gather | solution.py:59
  140.4 12.7 %fusion.64 = bf16[6,720,4,512]{3,2,1,0:T(4,128)(2,1)} fusion(bf16[6,720,4,512]{3,2,1,0:T(4,128)(2,1)} %get-tuple-element.157, s32[]{:T(128)} %get-tuple-element.156, f32[4,720,512]{2,0,1:T(4,128)} %fusion.62, f32[4,720,512]{2,0,1:T(4,128)} %fusion.63, bf16[8,720,512]{2,1,0:T(8,128)(2,1)} %bitcast.75, pred[8,720]{0,1:T(8,128)(4,1)S(1)} %copy.66, ...), kind=kOutput, calls=%fused_computation.15.clone.1 | convolution fusion | flops 30965760 | bytes 20650304 | tf_op jit(solution)/shard_map/while/body/eval_jaxpr/sjc,sk->jkc/dot_general | solution.py:60
  159.7 19.5 %gather_fusion.1 = bf16[5760,512]{1,0:T(8,128)(2,1)} fusion(bf16[2232,512]{1,0:T(8,128)(2,1)} %bitcast.71, s32[6144]{0:T(1024)S(1)} %pad_clamp_fusion.7), kind=kCustom, calls=%fused_computation.1.clone.clone.1 | custom fusion | bytes 11819520 | tf_op jit(solution)/shard_map/while/body/eval_jaxpr/jit(_take)/gather | solution.py:59
  191.8 19.5 %gather_fusion = bf16[5760,512]{1,0:T(8,128)(2,1)} fusion(bf16[2232,512]{1,0:T(8,128)(2,1)} %bitcast.72, s32[6144]{0:T(1024)S(1)} %pad_clamp_fusion.6), kind=kCustom, calls=%fused_computation.2.clone.clone.1 | custom fusion | bytes 11819520 | tf_op jit(solution)/shard_map/while/body/eval_jaxpr/jit(_take)/gather | solution.py:59
  223.1 19.5 %gather_fusion.2 = bf16[5760,512]{1,0:T(8,128)(2,1)} fusion(bf16[2232,512]{1,0:T(8,128)(2,1)} %bitcast.73, s32[6144]{0:T(1024)S(1)} %pad_clamp_fusion.8), kind=kCustom, calls=%fused_computation.clone.clone.1 | custom fusion | bytes 11819520 | tf_op jit(solution)/shard_map/while/body/eval_jaxpr/jit(_take)/gather | solution.py:59
  242.7 12.7 %fusion.64 = bf16[6,720,4,512]{3,2,1,0:T(4,128)(2,1)} fusion(bf16[6,720,4,512]{3,2,1,0:T(4,128)(2,1)} %get-tuple-element.157, s32[]{:T(128)} %get-tuple-element.156, f32[4,720,512]{2,0,1:T(4,128)} %fusion.62, f32[4,720,512]{2,0,1:T(4,128)} %fusion.63, bf16[8,720,512]{2,1,0:T(8,128)(2,1)} %bitcast.75, pred[8,720]{0,1:T(8,128)(4,1)S(1)} %copy.66, ...), kind=kOutput, calls=%fused_computation.15.clone.1 | convolution fusion | flops 30965760 | bytes 20650304 | tf_op jit(solution)/shard_map/while/body/eval_jaxpr/sjc,sk->jkc/dot_general | solution.py:60
  262.1 19.5 %gather_fusion.1 = bf16[5760,512]{1,0:T(8,128)(2,1)} fusion(bf16[2232,512]{1,0:T(8,128)(2,1)} %bitcast.71, s32[6144]{0:T(1024)S(1)} %pad_clamp_fusion.7), kind=kCustom, calls=%fused_computation.1.clone.clone.1 | custom fusion | bytes 11819520 | tf_op jit(solution)/shard_map/while/body/eval_jaxpr/jit(_take)/gather | solution.py:59
  294.2 19.5 %gather_fusion = bf16[5760,512]{1,0:T(8,128)(2,1)} fusion(bf16[2232,512]{1,0:T(8,128)(2,1)} %bitcast.72, s32[6144]{0:T(1024)S(1)} %pad_clamp_fusion.6), kind=kCustom, calls=%fused_computation.2.clone.clone.1 | custom fusion | bytes 11819520 | tf_op jit(solution)/shard_map/while/body/eval_jaxpr/jit(_take)/gather | solution.py:59
  325.5 19.5 %gather_fusion.2 = bf16[5760,512]{1,0:T(8,128)(2,1)} fusion(bf16[2232,512]{1,0:T(8,128)(2,1)} %bitcast.73, s32[6144]{0:T(1024)S(1)} %pad_clamp_fusion.8), kind=kCustom, calls=%fused_computation.clone.clone.1 | custom fusion | bytes 11819520 | tf_op jit(solution)/shard_map/while/body/eval_jaxpr/jit(_take)/gather | solution.py:59
  345.1 12.8 %fusion.64 = bf16[6,720,4,512]{3,2,1,0:T(4,128)(2,1)} fusion(bf16[6,720,4,512]{3,2,1,0:T(4,128)(2,1)} %get-tuple-element.157, s32[]{:T(128)} %get-tuple-element.156, f32[4,720,512]{2,0,1:T(4,128)} %fusion.62, f32[4,720,512]{2,0,1:T(4,128)} %fusion.63, bf16[8,720,512]{2,1,0:T(8,128)(2,1)} %bitcast.75, pred[8,720]{0,1:T(8,128)(4,1)S(1)} %copy.66, ...), kind=kOutput, calls=%fused_computation.15.clone.1 | convolution fusion | flops 30965760 | bytes 20650304 | tf_op jit(solution)/shard_map/while/body/eval_jaxpr/sjc,sk->jkc/dot_general | solution.py:60
  364.6 19.5 %gather_fusion.1 = bf16[5760,512]{1,0:T(8,128)(2,1)} fusion(bf16[2232,512]{1,0:T(8,128)(2,1)} %bitcast.71, s32[6144]{0:T(1024)S(1)} %pad_clamp_fusion.7), kind=kCustom, calls=%fused_computation.1.clone.clone.1 | custom fusion | bytes 11819520 | tf_op jit(solution)/shard_map/while/body/eval_jaxpr/jit(_take)/gather | solution.py:59
  396.6 19.5 %gather_fusion = bf16[5760,512]{1,0:T(8,128)(2,1)} fusion(bf16[2232,512]{1,0:T(8,128)(2,1)} %bitcast.72, s32[6144]{0:T(1024)S(1)} %pad_clamp_fusion.6), kind=kCustom, calls=%fused_computation.2.clone.clone.1 | custom fusion | bytes 11819520 | tf_op jit(solution)/shard_map/while/body/eval_jaxpr/jit(_take)/gather | solution.py:59
  427.9 19.5 %gather_fusion.2 = bf16[5760,512]{1,0:T(8,128)(2,1)} fusion(bf16[2232,512]{1,0:T(8,128)(2,1)} %bitcast.73, s32[6144]{0:T(1024)S(1)} %pad_clamp_fusion.8), kind=kCustom, calls=%fused_computation.clone.clone.1 | custom fusion | bytes 11819520 | tf_op jit(solution)/shard_map/while/body/eval_jaxpr/jit(_take)/gather | solution.py:59
  447.6 12.7 %fusion.64 = bf16[6,720,4,512]{3,2,1,0:T(4,128)(2,1)} fusion(bf16[6,720,4,512]{3,2,1,0:T(4,128)(2,1)} %get-tuple-element.157, s32[]{:T(128)} %get-tuple-element.156, f32[4,720,512]{2,0,1:T(4,128)} %fusion.62, f32[4,720,512]{2,0,1:T(4,128)} %fusion.63, bf16[8,720,512]{2,1,0:T(8,128)(2,1)} %bitcast.75, pred[8,720]{0,1:T(8,128)(4,1)S(1)} %copy.66, ...), kind=kOutput, calls=%fused_computation.15.clone.1 | convolution fusion | flops 30965760 | bytes 20650304 | tf_op jit(solution)/shard_map/while/body/eval_jaxpr/sjc,sk->jkc/dot_general | solution.py:60
  466.9 19.5 %gather_fusion.1 = bf16[5760,512]{1,0:T(8,128)(2,1)} fusion(bf16[2232,512]{1,0:T(8,128)(2,1)} %bitcast.71, s32[6144]{0:T(1024)S(1)} %pad_clamp_fusion.7), kind=kCustom, calls=%fused_computation.1.clone.clone.1 | custom fusion | bytes 11819520 | tf_op jit(solution)/shard_map/while/body/eval_jaxpr/jit(_take)/gather | solution.py:59
  499.0 19.5 %gather_fusion = bf16[5760,512]{1,0:T(8,128)(2,1)} fusion(bf16[2232,512]{1,0:T(8,128)(2,1)} %bitcast.72, s32[6144]{0:T(1024)S(1)} %pad_clamp_fusion.6), kind=kCustom, calls=%fused_computation.2.clone.clone.1 | custom fusion | bytes 11819520 | tf_op jit(solution)/shard_map/while/body/eval_jaxpr/jit(_take)/gather | solution.py:59
  530.3 19.5 %gather_fusion.2 = bf16[5760,512]{1,0:T(8,128)(2,1)} fusion(bf16[2232,512]{1,0:T(8,128)(2,1)} %bitcast.73, s32[6144]{0:T(1024)S(1)} %pad_clamp_fusion.8), kind=kCustom, calls=%fused_computation.clone.clone.1 | custom fusion | bytes 11819520 | tf_op jit(solution)/shard_map/while/body/eval_jaxpr/jit(_take)/gather | solution.py:59
  550.0 12.7 %fusion.64 = bf16[6,720,4,512]{3,2,1,0:T(4,128)(2,1)} fusion(bf16[6,720,4,512]{3,2,1,0:T(4,128)(2,1)} %get-tuple-element.157, s32[]{:T(128)} %get-tuple-element.156, f32[4,720,512]{2,0,1:T(4,128)} %fusion.62, f32[4,720,512]{2,0,1:T(4,128)} %fusion.63, bf16[8,720,512]{2,1,0:T(8,128)(2,1)} %bitcast.75, pred[8,720]{0,1:T(8,128)(4,1)S(1)} %copy.66, ...), kind=kOutput, calls=%fused_computation.15.clone.1 | convolution fusion | flops 30965760 | bytes 20650304 | tf_op jit(solution)/shard_map/while/body/eval_jaxpr/sjc,sk->jkc/dot_general | solution.py:60
  569.3 19.5 %gather_fusion.1 = bf16[5760,512]{1,0:T(8,128)(2,1)} fusion(bf16[2232,512]{1,0:T(8,128)(2,1)} %bitcast.71, s32[6144]{0:T(1024)S(1)} %pad_clamp_fusion.7), kind=kCustom, calls=%fused_computation.1.clone.clone.1 | custom fusion | bytes 11819520 | tf_op jit(solution)/shard_map/while/body/eval_jaxpr/jit(_take)/gather | solution.py:59
  601.3 19.5 %gather_fusion = bf16[5760,512]{1,0:T(8,128)(2,1)} fusion(bf16[2232,512]{1,0:T(8,128)(2,1)} %bitcast.72, s32[6144]{0:T(1024)S(1)} %pad_clamp_fusion.6), kind=kCustom, calls=%fused_computation.2.clone.clone.1 | custom fusion | bytes 11819520 | tf_op jit(solution)/shard_map/while/body/eval_jaxpr/jit(_take)/gather | solution.py:59
  632.6 19.5 %gather_fusion.2 = bf16[5760,512]{1,0:T(8,128)(2,1)} fusion(bf16[2232,512]{1,0:T(8,128)(2,1)} %bitcast.73, s32[6144]{0:T(1024)S(1)} %pad_clamp_fusion.8), kind=kCustom, calls=%fused_computation.clone.clone.1 | custom fusion | bytes 11819520 | tf_op jit(solution)/shard_map/while/body/eval_jaxpr/jit(_take)/gather | solution.py:59
  652.3 12.7 %fusion.64 = bf16[6,720,4,512]{3,2,1,0:T(4,128)(2,1)} fusion(bf16[6,720,4,512]{3,2,1,0:T(4,128)(2,1)} %get-tuple-element.157, s32[]{:T(128)} %get-tuple-element.156, f32[4,720,512]{2,0,1:T(4,128)} %fusion.62, f32[4,720,512]{2,0,1:T(4,128)} %fusion.63, bf16[8,720,512]{2,1,0:T(8,128)(2,1)} %bitcast.75, pred[8,720]{0,1:T(8,128)(4,1)S(1)} %copy.66, ...), kind=kOutput, calls=%fused_computation.15.clone.1 | convolution fusion | flops 30965760 | bytes 20650304 | tf_op jit(solution)/shard_map/while/body/eval_jaxpr/sjc,sk->jkc/dot_general | solution.py:60
  665.0 12.0 %copy.46 = bf16[540,8,4,512]{3,1,2,0:T(8,128)(2,1)S(1)} copy(bf16[540,8,4,512]{3,2,1,0:T(4,128)(2,1)} %bitcast.78) | data formatting | bytes 35389440
  677.0 29.3 %fusion.28 = bf16[4320,512]{1,0:T(8,128)(2,1)} fusion(bf16[4320,2048]{1,0:T(8,128)(2,1)S(1)} %bitcast.79, bf16[2048,512]{1,0:T(8,128)(2,1)S(1)} %bitcast.70), kind=kOutput, calls=%fused_computation.49 | convolution fusion | flops 9203466240 | bytes 24215552 | tf_op jit(solution)/shard_map/dot_general | solution.py:81
  715.0 15.0 %all_to_all.36 = bf16[6,720,512]{1,0,2:T(8,128)(2,1)} all-to-all(bf16[6,720,512]{1,0,2:T(8,128)(2,1)} %copy.40), channel_id=1, replica_groups=mesh['lat'=64,'lon'=2] {'lon'}, dimensions={2} | all-to-all | bytes 8847360 | tf_op jit(solution)/shard_map/all_to_all | solution.py:93
  755.1 63.2 %all_to_all.37 = bf16[2,640,6,256]{3,0,2,1:T(2,128)(2,1)} all-to-all(bf16[2,640,6,256]{3,0,2,1:T(2,128)(2,1)S(1)} %copy.42), channel_id=1, replica_groups=mesh['lat'=64,'lon'=2] {'lat'}, dimensions={1} | all-to-all | bytes 7864320 | tf_op jit(solution)/shard_map/all_to_all | solution.py:97
  (140 shorter events, 216.4 us)
Async XLA Ops:
  0.0 677.0 %copy-start = (bf16[4,512,512]{2,1,0:T(8,128)(2,1)S(1)}, bf16[4,512,512]{2,1,0:T(8,128)(2,1)}, u32[]{:S(2)}) copy-start(bf16[4,512,512]{2,1,0:T(8,128)(2,1)} %param.15) | copy-start | bytes 6291460
  0.0 24.9 %copy-start.2 = (bf16[6,720,512]{2,1,0:T(8,128)(2,1)S(1)}, bf16[6,720,512]{2,1,0:T(8,128)(2,1)}, u32[]{:S(2)}) copy-start(bf16[6,720,512]{2,1,0:T(8,128)(2,1)} %param.10) | copy-start | bytes 13271044
  1.6 23.2 %collective-permute-start = (bf16[1,720,512]{2,1,0:T(8,128)(2,1)S(1)}, bf16[1,720,512]{2,1,0:T(8,128)(2,1)S(1)}, u32[]{:S(2)}, u32[]{:S(2)}) collective-permute-start(bf16[1,720,512]{2,1,0:T(8,128)(2,1)S(1)} %get-tuple-element.88), channel_id=1, source_target_pairs={{0,2},{2,4},{4,6},{6,8},{8,10},{10,12},{12,14},{14,16},{16,18},{18... | collective-permute-start | bytes 2211848 | tf_op jit(solution)/shard_map/ppermute | solution.py:19
  5.9 19.7 %collective-permute-start.1 = (bf16[1,720,512]{2,1,0:T(8,128)(2,1)S(1)}, bf16[1,720,512]{2,1,0:T(8,128)(2,1)S(1)}, u32[]{:S(2)}, u32[]{:S(2)}) collective-permute-start(bf16[1,720,512]{2,1,0:T(8,128)(2,1)S(1)} %get-tuple-element.87), channel_id=1, source_target_pairs={{2,0},{4,2},{6,4},{8,6},{10,8},{12,10},{14,12},{16,14},{18,16},{20... | collective-permute-start | bytes 2211848 | tf_op jit(solution)/shard_map/ppermute | solution.py:22
  24.8 4.6 copy-start.3
  24.8 4.6 copy-start.4
  25.6 2.5 copy-start.1
  28.1 2.2 collective-permute-start.2
  29.3 1.3 collective-permute-start.3
where the time goes:
time: 832 us; the launch traced here: 827 us
  local copies, waits for them, and re-layouts  431 us (52%)
  matrix products  254 us (31%)
  blocking collectives  78.2 us (9%)
  other arithmetic  31.4 us (4%)
  loops' own time  23.4 us (3%)
    gather x18, local copies, waits for them, and re-layouts, one_row(): picked = jnp.take(flat_window, flat_index[first:last], axis=0)  350 us
    dot_general x18, matrix products, one_row(): jnp.einsum('sjc,sk->jkc', picked, basis_row[first:last], preferred_elemen...  214 us
    all_to_all x1, blocking collectives, body(): return lax.all_to_all(zonal, 'lat', split_axis=1, concat_axis=2, tiled=True)  63.2 us
    dot_general x1, matrix products, body(): jnp.dot(aggregated.reshape(lat_rows * lon_cols, K * channels), mix_weight...  29.3 us
    another operation x1, loops' own time, aggregate_block(): lax.map(one_row, (jnp.arange(lat_rows, dtype=jnp.int32), support_lat, lon...  23.4 us
    dynamic_slice x6, local copies, waits for them, and re-layouts, one_row(): lax.dynamic_slice(extended, (row_index, col_start - HMAX, jnp.int32(0)),...  19.3 us
    another operation x1, other arithmetic  17 us
  transfers between devices with their start and end apart: 4, of which 2 were waited for; matrix products, arithmetic and copies ran while one was open for 2% of the time, Pallas kernels for 0%

commit v1 on v0

v1 whole, which is shorter than its diff:
```python
import functools

import jax
import jax.numpy as jnp
import ml_dtypes
import numpy as np
from jax import lax
from jax.experimental import pallas as pl
from jax.experimental.pallas import tpu as pltpu
from jax.sharding import PartitionSpec as P

MMAX = 640
K = 4
RLAT = 1
HMAX = 12
EDGE = 16
COLS = 48
SPAN = COLS + 2 * EDGE
DEPTH = 256
VMEM = 60 * 1024 * 1024


def exact_gelu(x):
    return 0.5 * x * (1.0 + lax.erf(x * 0.7071067811865476))


def conv_kernel(row_step, sources, table_rows, table_ref, own_ref, mix_hbm, *refs):
    ins, (keep_ref, send_ref, ext, agg, band, mix_ref, sems, mix_sem) = refs[:-8], refs[-8:]
    step = pl.program_id(0)
    support = table_ref.shape[1] // (K + 1)
    lon_cols = keep_ref.shape[1]
    channels = ext.shape[2]
    half = channels // 2
    ext_rows = ext.shape[0]
    steps = (ext_rows - 3) // row_step + 1
    mix_copy = pltpu.make_async_copy(mix_hbm, mix_ref, mix_sem)

    def copies(row):
        pieces = []
        for n, (ref, i, start, size, at) in enumerate(sources[row]):
            pieces.append(
                pltpu.make_async_copy(
                    ins[ref].at[i, pl.ds(start, size)], ext.at[row, pl.ds(at, size)], sems.at[row, n]
                )
            )
        return pieces

    def wait_rows(first, last):
        for row in range(first, last):
            for copy in copies(row):
                copy.wait()

    @pl.when(step == 0)
    def _():
        for row in range(ext_rows):
            for copy in copies(row):
                copy.start()
            if row == 2:
                mix_copy.start()
        wait_rows(0, 3)

    for later in range(1, steps):
        @pl.when(step == later)
        def _(later=later):
            wait_rows(3 + row_step * (later - 1), 3 + row_step * later)

    base = step * row_step
    here = table_rows[0] + step * table_rows[1]

    lanes = lax.broadcasted_iota(jnp.int32, (8, DEPTH), 1).astype(jnp.float32)
    filters = [jnp.zeros((8, DEPTH), jnp.float32) for _ in range(K)]
    for s in range(support):
        hit = lanes == table_ref[here, s]
        for k in range(K):
            filters[k] = filters[k] + jnp.where(hit, table_ref[here, support + s * K + k], 0.0)
    for k in range(K):
        for q in range(0, COLS, 16):
            pair = [
                pltpu.roll(filters[k], q + e, 1, stride=1, stride_axis=0) for e in (0, 8)
            ]
            band[pl.ds(k * COLS + q, 16), :] = jnp.concatenate(pair, axis=0).astype(jnp.bfloat16)

    for start in range(0, lon_cols, COLS):
        window = jnp.concatenate(
            [ext[base + r, pl.ds(start, SPAN), :] for r in range(3)]
            + [ext[base, pl.ds(start, DEPTH - 3 * SPAN), :]],
            axis=0,
        )
        got = jnp.dot(band[...], window, preferred_element_type=jnp.float32).astype(jnp.bfloat16)
        for k in range(K):
            agg[pl.ds(start, COLS), pl.ds(k * channels, channels)] = got[k * COLS : (k + 1) * COLS]

    @pl.when(step == 0)
    def _():
        mix_copy.wait()

    own = own_ref[0]
    for out, part in ((send_ref, 1 - own), (keep_ref, own)):
        weights = mix_ref[:, pl.ds(pl.multiple_of(part * half, half), half)]
        conv = jnp.dot(agg[...], weights, preferred_element_type=jnp.float32)
        out[0] = exact_gelu(conv).astype(out.dtype)


def convolve(row_step, steps, sources, table_rows, table, own, mix, arrays):
    lon_cols, channels = arrays[0].shape[1:]
    smem = pl.BlockSpec(memory_space=pltpu.SMEM)
    hbm = pl.BlockSpec(memory_space=pl.ANY)
    out = jax.ShapeDtypeStruct((steps, lon_cols, channels // 2), jnp.bfloat16)
    out_spec = pl.BlockSpec((1, lon_cols, channels // 2), lambda i: (i, 0, 0))
    ext_rows = len(sources)
    return pl.pallas_call(
        functools.partial(conv_kernel, row_step, sources, table_rows),
        grid=(steps,),
        in_specs=[smem, smem, hbm] + [hbm] * len(arrays),
        out_specs=[out_spec, out_spec],
        out_shape=[out, out],
        scratch_shapes=[
            pltpu.VMEM((ext_rows, lon_cols + 2 * EDGE, channels), jnp.bfloat16),
            pltpu.VMEM((lon_cols, K * channels), jnp.bfloat16),
            pltpu.VMEM((K * COLS, DEPTH), jnp.bfloat16),
            pltpu.VMEM(mix.shape, jnp.bfloat16),
            pltpu.SemaphoreType.DMA((ext_rows, 3)),
            pltpu.SemaphoreType.DMA,
        ],
        compiler_params=pltpu.CompilerParams(
            dimension_semantics=("arbitrary",), vmem_limit_bytes=VMEM
        ),
        cost_estimate=pl.CostEstimate(
            flops=2 * steps * lon_cols * channels * (K * channels + 4 * 256),
            bytes_accessed=2 * (ext_rows + steps) * lon_cols * channels + 2 * mix.size,
            transcendentals=0,
        ),
        name="convolve",
    )(table, own, mix, *arrays)


def twiddles(total_lon, groups):
    half = total_lon // 2
    per = MMAX // groups
    cols = np.arange(half, dtype=np.int64)
    tables = []
    for parity in (0, 1):
        modes = (np.arange(groups)[:, None] * per + np.arange(per // 2)[None, :] * 2 + parity)
        turn = (modes[:, :, None] * cols) % total_lon
        angles = turn.astype(np.float32) * np.float32(2.0 * np.pi / total_lon)
        scale = np.float32(1.0) / np.sqrt(np.float32(total_lon))
        both = np.stack([np.cos(angles) * scale, -np.sin(angles) * scale], axis=1)
        table = np.zeros((MMAX, -(-half // 256) * 256), np.float32)
        table[:, :half] = both.reshape(MMAX, half)
        tables.append(table.astype(ml_dtypes.bfloat16))
    return tables


def zonal_kernel(lats, groups, sign_ref, even_hbm, odd_hbm, ka, ra, kb, rb, out_hbm, *scratch):
    even_ref, odd_ref, keep, recv, lo, hi, out, sems, table_sems, out_sems = scratch
    rows, half, width = keep.shape
    rows_a = ka.shape[0]
    tables = (
        pltpu.make_async_copy(even_hbm, even_ref, table_sems.at[0]),
        pltpu.make_async_copy(odd_hbm, odd_ref, table_sems.at[1]),
    )
    copies = []
    for i in range(rows):
        sides = ((ka, ra), i) if i < rows_a else ((kb, rb), i - rows_a)
        copies.append(
            [
                pltpu.make_async_copy(ref.at[sides[1]], held.at[i], sems.at[i, n])
                for n, (ref, held) in enumerate(zip(sides[0], (keep, recv)))
            ]
        )
    for i in range(rows):
        for copy in copies[i]:
            copy.start()
        if i < 2:
            tables[i].start()

    pad = jnp.zeros((even_ref.shape[1] - half, 2 * width), jnp.bfloat16)
    for i in range(0, rows, 2):
        for copy in copies[i] + copies[i + 1]:
            copy.wait()
        x, y = (
            jnp.concatenate([held[i], held[i + 1]], axis=1).astype(jnp.float32)
            for held in (keep, recv)
        )
        for parity, table, value in ((0, even_ref, x + y), (1, odd_ref, (x - y) * sign_ref[0])):
            if i == 0:
                tables[parity].wait()
            folded = jnp.concatenate([value.astype(jnp.bfloat16), pad], axis=0)
            got = jnp.dot(table[...], folded, preferred_element_type=jnp.float32)
            for e in (0, 1):
                where = pl.ds(parity * rows + lats[i + e], MMAX, stride=2 * rows)
                lo[where, :] = got[:, e * width : e * width + 128]
                hi[where, :] = got[:, e * width + 128 : (e + 1) * width]

    size = out.shape[1]
    batch = groups // out_sems.shape[0]

    def send(b):
        at = pl.ds(b * batch, batch)
        return pltpu.make_async_copy(out.at[at], out_hbm.at[at], out_sems.at[b])

    for b in range(out_sems.shape[0]):
        for g in range(b * batch, (b + 1) * batch):
            at = pl.ds(g * size, size)
            out[g, :, pl.ds(0, 128)] = lo[at, :].astype(out.dtype)
            out[g, :, pl.ds(128, 128)] = hi[at, :].astype(out.dtype)
        send(b).start()
    for b in range(out_sems.shape[0]):
        send(b).wait()


def zonal(sign, keep_a, recv_a, keep_b, recv_b, lats, groups):
    rows_a, half, width = keep_a.shape
    rows = rows_a + keep_b.shape[0]
    even, odd = (jnp.asarray(t) for t in twiddles(2 * half, groups))
    hbm = pl.BlockSpec(memory_space=pl.ANY)
    block = (groups, 2 * MMAX // groups * rows, width)
    return pl.pallas_call(
        functools.partial(zonal_kernel, lats, groups),
        in_specs=[pl.BlockSpec(memory_space=pltpu.SMEM)] + [hbm] * 6,
        out_specs=hbm,
        out_shape=jax.ShapeDtypeStruct(block, jnp.bfloat16),
        scratch_shapes=[
            pltpu.VMEM(even.shape, jnp.bfloat16),
            pltpu.VMEM(odd.shape, jnp.bfloat16),
            pltpu.VMEM((rows, half, width), jnp.bfloat16),
            pltpu.VMEM((rows, half, width), jnp.bfloat16),
            pltpu.VMEM((2 * MMAX * rows, 128), jnp.float32),
            pltpu.VMEM((2 * MMAX * rows, 128), jnp.float32),
            pltpu.VMEM(block, jnp.bfloat16),
            pltpu.SemaphoreType.DMA((rows, 2)),
            pltpu.SemaphoreType.DMA((2,)),
            pltpu.SemaphoreType.DMA((8,)),
        ],
        compiler_params=pltpu.CompilerParams(vmem_limit_bytes=VMEM),
        cost_estimate=pl.CostEstimate(
            flops=4 * rows * MMAX * even.shape[1] * width,
            bytes_accessed=2 * (2 * rows * half * width + 2 * even.size + 2 * MMAX * rows * width),
            transcendentals=0,
        ),
        name="zonal",
    )(sign, even, odd, keep_a, recv_a, keep_b, recv_b)


def gather_kernel(rows, in_ref, out_ref, wide, laid):
    sources, size, width = in_ref.shape
    modes = size // rows
    for c in range(0, width, 128):
        at = pl.ds(c, 128)
        for g in range(sources):
            wide[pl.ds(g * size, size), :] = in_ref[g, :, at].astype(jnp.float32)
        for m in range(modes):
            for i in range(rows):
                piece = wide[pl.ds(m * rows + i, sources, stride=size), :]
                laid[pl.ds(m * sources * rows + i, sources, stride=rows), :] = piece
        for m in range(modes):
            out_ref[m, :, at] = laid[pl.ds(m * sources * rows, sources * rows), :].astype(out_ref.dtype)


def gather(moved, rows):
    bands, size, width = moved.shape
    batch = 8
    modes = size // rows
    return pl.pallas_call(
        functools.partial(gather_kernel, rows),
        grid=(bands // batch,),
        in_specs=[pl.BlockSpec((batch, size, width), lambda g: (g, 0, 0))],
        out_specs=pl.BlockSpec((modes, batch * rows, width), lambda g: (0, g, 0)),
        out_shape=jax.ShapeDtypeStruct((modes, bands * rows, width), moved.dtype),
        scratch_shapes=[
            pltpu.VMEM((batch * size, 128), jnp.float32),
            pltpu.VMEM((batch * size, 128), jnp.float32),
        ],
        compiler_params=pltpu.CompilerParams(
            dimension_semantics=("arbitrary",), vmem_limit_bytes=VMEM
        ),
        name="gather",
    )(moved)


def body(grid_field, basis_values, support_lat, support_lon, lon_reach, mix_weights):
    lat_rows, lon_cols, channels = grid_field.shape
    bands = lax.axis_size("lat")
    own = lax.axis_index("lon")
    swap = [(0, 1), (1, 0)]
    ahead = [(i, i + 1) for i in range(bands - 1)]
    back = [(b, a) for a, b in ahead]
    last = lat_rows - 1

    edge = jnp.concatenate([grid_field[:, :EDGE], grid_field[:, lon_cols - EDGE :]], axis=1)
    edges = lax.ppermute(edge, "lon", swap)

    def wide_row(row):
        return jnp.concatenate(
            [edges[row, EDGE:], grid_field[row], edges[row, :EDGE]], axis=0
        )[None]

    low = lax.ppermute(wide_row(last), "lat", ahead)
    high = lax.ppermute(wide_row(0), "lat", back)

    shift = jnp.clip(support_lon, -lon_reach[:, None], lon_reach[:, None])
    index = ((support_lat + RLAT) * SPAN + EDGE + shift).astype(jnp.float32)
    basis = basis_values.astype(jnp.float32).reshape(lat_rows, -1)
    table = jnp.concatenate([index, basis], axis=1)
    mix = mix_weights.reshape(K * channels, channels)
    own_1 = own.astype(jnp.int32).reshape(1)

    def own_row(row):
        return (
            (0, row, 0, lon_cols, EDGE),
            (1, row, EDGE, EDGE, 0),
            (1, row, 0, EDGE, EDGE + lon_cols),
        )

    def beside(ref):
        return ((ref, 0, 0, lon_cols + 2 * EDGE, 0),)

    keep_a, send_a = convolve(
        1, lat_rows - 2, [own_row(r) for r in range(lat_rows)], (1, 1), table, own_1, mix,
        [grid_field, edges],
    )
    recv_a = lax.ppermute(send_a, "lon", swap)
    outer = [beside(2), own_row(0), own_row(1), own_row(last - 1), own_row(last), beside(3)]
    keep_b, send_b = convolve(
        3, 2, outer, (0, last), table, own_1, mix, [grid_field, edges, low, high]
    )
    recv_b = lax.ppermute(send_b, "lon", swap)
    sign = (1 - 2 * own).astype(jnp.float32).reshape(1)
    lats = list(range(1, last)) + [0, last]
    packed = zonal(sign, keep_a, recv_a, keep_b, recv_b, lats, bands)
    moved = lax.all_to_all(packed, "lat", 0, 0, tiled=True)
    out = gather(moved, lat_rows)
    return out.reshape(2, MMAX // bands, bands * lat_rows, channels // 2)


def solution(mesh):
    return jax.shard_map(
        body,
        mesh=mesh,
        in_specs=(
            P("lat", "lon", None),
            P("lat", None, None),
            P("lat", None),
            P("lat", None),
            P("lat"),
            P(),
        ),
        out_specs=P(None, "lat", None, "lon"),
        check_vma=False,
    )
```

time: 832 us -> 124 us (0.15)
  local copies, waits for them, and re-layouts: 431 us -> 4.17 us
  matrix products: 254 us -> 0 us
  Pallas kernels: 0 us -> 40.1 us
  other arithmetic: 31.4 us -> 2.22 us
  loops' own time: 23.4 us -> 0 us
  blocking collectives: 78.2 us -> 62.4 us
    gather x18 -> x0, local copies, waits for them, and re-layouts: 350 us -> none  [one_row(): picked = jnp.take(flat_window, flat_index[first:last], axis=0)]
    dot_general x20 -> x0, matrix products: 254 us -> none  [the longest x18 214 us: one_row(): jnp.einsum('sjc,sk->jkc', picked, basis_row[first:last], preferred_elemen...]
    pallas_call x0 -> x4, Pallas kernels: none -> 40.1 us  [the longest x2 24.6 us: convolve(): pl.pallas_call(functools.partial(conv_kernel, row_step, sources, table_ro...]
    dynamic_slice x18 -> x0, local copies, waits for them, and re-layouts: 26.9 us -> none  [the longest x6 19.3 us: one_row(): lax.dynamic_slice(extended, (row_index, col_start - HMAX, jnp.int32(0)),...]
    another operation x1 -> x0, loops' own time: 23.4 us -> none  [aggregate_block(): lax.map(one_row, (jnp.arange(lat_rows, dtype=jnp.int32), support_lat, lon...]
    another operation x1 -> x0, other arithmetic: 17 us -> none
    all_to_all x3 -> x0, local copies, waits for them, and re-layouts: 16.2 us -> none  [the longest x1 8.29 us: body(): lax.all_to_all(activated, 'lon', split_axis=2, concat_axis=1, tiled=True)]
    all_to_all x2 -> x1, blocking collectives: 78.2 us -> 62.4 us  [body(): moved = lax.all_to_all(packed, 'lat', 0, 0, tiled=True)]
  transfers between devices with their start and end apart: 4 -> 5, of which waited for: 2 -> 2; matrix products, arithmetic and copies ran while one was open for 2% -> 4% of each run, Pallas kernels for 0% -> 20%
where the time goes in v1:
time: 124 us; the launch traced here: 123 us
  blocking collectives  62.4 us (50%)
  Pallas kernels  40.1 us (32%)
  starting transfers between devices  8.51 us (7%)
  waiting for transfers between devices  5.49 us (4%)
  local copies, waits for them, and re-layouts  4.17 us (3%)
  other arithmetic  2.22 us (2%)
    all_to_all x1, blocking collectives, body(): moved = lax.all_to_all(packed, 'lat', 0, 0, tiled=True)  62.4 us
    pallas_call x2, Pallas kernels, convolve(): pl.pallas_call(functools.partial(conv_kernel, row_step, sources, table_ro...  24.6 us
    pallas_call x1, Pallas kernels, zonal(): pl.pallas_call(functools.partial(zonal_kernel, lats, groups), in_specs=[p...  8.15 us
    pallas_call x1, Pallas kernels, gather(): pl.pallas_call(functools.partial(gather_kernel, rows), grid=(bands // bat...  7.4 us
    ppermute x1, starting transfers between devices, body(): low = lax.ppermute(wide_row(last), 'lat', ahead)  4.1 us
    ppermute x1, waiting for transfers between devices, body(): high = lax.ppermute(wide_row(0), 'lat', back)  3.44 us
  transfers between devices with their start and end apart: 5, of which 2 were waited for; matrix products, arithmetic and copies ran while one was open for 4% of the time, Pallas kernels for 20%

profile of v1, /device:TPU:1, one launch (start us, length us, event | category | flops | bytes accessed | tf_op | source)
XLA Modules:
  0.0 123.0 jit_solution(175834734680492936)
XLA Ops:
  0.0 1.0 fusion
  1.0 1.5 %collective-permute-start = (bf16[6,32,512]{2,1,0:T(8,128)(2,1)S(1)}, bf16[6,32,512]{2,1,0:T(8,128)(2,1)S(1)}, u32[]{:S(2)}, u32[]{:S(2)}) collective-permute-start(bf16[6,32,512]{2,1,0:T(8,128)(2,1)S(1)} %pad_maximum_fusion), channel_id=1, source_target_pairs={{0,1},{1,0},{2,3},{3,2},{4,5},{5,4},{6,7},{7,6},{8,9},{9,8},{10,11... | collective-permute-start | bytes 589832 | tf_op jit(solution)/shard_map/ppermute | solution.py:291
  2.5 0.7 neg.4
  3.1 0.8 copy.10
  3.9 0.1 reshape.28
  4.0 0.8 add_convert_fusion
  4.8 0.7 pad_maximum_fusion.1.table_ref
  5.5 1.4 %slice_bitcast_fusion = (bf16[720,512]{1,0:T(8,128)(2,1)S(1)}, bf16[720,512]{1,0:T(8,128)(2,1)S(1)}) fusion(bf16[6,720,512]{2,1,0:T(8,128)(2,1)} %refs_0_.3), kind=kLoop, calls=%fused_computation.2 | loop fusion | bytes 2949120 | tf_op jit(solution)/shard_map/squeeze | solution.py:295
  6.9 0.0 collective-permute-done.refs_1_
  6.9 0.0 copy-start
  7.0 0.1 maximum_bitcast_fusion
  7.0 4.1 %collective-permute-start.2 = (bf16[1,752,512]{2,1,0:T(8,128)(2,1)S(1)}, bf16[1,752,512]{2,1,0:T(8,128)(2,1)}, u32[]{:S(2)}, u32[]{:S(2)}) collective-permute-start(bf16[1,752,512]{2,1,0:T(8,128)(2,1)S(1)} %maximum_bitcast_fusion), channel_id=1, source_target_pairs={{0,2},{2,4},{4,6},{6,8},{8,10},{10,12},{12,14},{14,16},{16,18},{18... | collective-permute-start | bytes 2310152 | tf_op jit(solution)/shard_map/ppermute | solution.py:298
  11.1 0.1 maximum_bitcast_fusion.1
  11.2 0.0 copy-done
  11.2 1.3 %collective-permute-start.3 = (bf16[1,752,512]{2,1,0:T(8,128)(2,1)S(1)}, bf16[1,752,512]{2,1,0:T(8,128)(2,1)}, u32[]{:S(2)}, u32[]{:S(2)}) collective-permute-start(bf16[1,752,512]{2,1,0:T(8,128)(2,1)S(1)} %maximum_bitcast_fusion.1), channel_id=1, source_target_pairs={{2,0},{4,2},{6,4},{8,6},{10,8},{12,10},{14,12},{16,14},{18,16},{20... | collective-permute-start | bytes 2310152 | tf_op jit(solution)/shard_map/ppermute | solution.py:299
  12.5 15.3 %convolve.2 = (bf16[4,720,256]{2,1,0:T(8,128)(2,1)}, bf16[4,720,256]{2,1,0:T(8,128)(2,1)}) custom-call(f32[6,120]{1,0:T(8,128)} %pad_maximum_fusion.1.table_ref, s32[1]{0:T(128)} %bitcast.1.own_ref, bf16[2048,512]{1,0:T(8,128)(2,1)} %bitcast.20, bf16[6,720,512]{2,1,0:T(8,128)(2,1)} %refs_0_.3, bf16[6,32,512]{2,1,0:T(8,128)(2,1)} %copy-done), custom_call_target="tpu_custom_call" | custom-call | flops 9059696640 | bytes 9469952 | tf_op jit(solution)/shard_map/convolve/pallas_call | solution.py:111
  27.8 0.4 collective-permute-start.1
  28.2 0.0 collective-permute-done.2.refs_2_
  28.2 3.4 %collective-permute-done.3.refs_3_ = bf16[1,752,512]{2,1,0:T(8,128)(2,1)} collective-permute-done((bf16[1,752,512]{2,1,0:T(8,128)(2,1)S(1)}, bf16[1,752,512]{2,1,0:T(8,128)(2,1)}, u32[]{:S(2)}, u32[]{:S(2)}) %collective-permute-start.3) | collective-permute-done | bytes 770080 | tf_op jit(solution)/shard_map/ppermute | solution.py:299
  31.7 9.2 %convolve.3 = (bf16[2,720,256]{2,1,0:T(8,128)(2,1)}, bf16[2,720,256]{2,1,0:T(8,128)(2,1)}) custom-call(f32[6,120]{1,0:T(8,128)} %pad_maximum_fusion.1.table_ref, s32[1]{0:T(128)} %bitcast.1.own_ref, bf16[2048,512]{1,0:T(8,128)(2,1)} %bitcast.21, bf16[6,720,512]{2,1,0:T(8,128)(2,1)} %refs_0_.3, bf16[6,32,512]{2,1,0:T(8,128)(2,1)} %copy-done, ...), custom_call_target="tpu_custom_call" | custom-call | flops 4529848320 | bytes 7995392 | tf_op jit(solution)/shard_map/convolve/pallas_call | solution.py:111
  40.9 1.2 collective-permute-start.4
  42.1 0.0 collective-permute-done.1.ra
  42.1 0.0 copy-start.1
  42.1 2.0 %collective-permute-done.4.rb = bf16[2,720,256]{2,1,0:T(8,128)(2,1)S(1)} collective-permute-done((bf16[2,720,256]{2,1,0:T(8,128)(2,1)}, bf16[2,720,256]{2,1,0:T(8,128)(2,1)S(1)}, u32[]{:S(2)}, u32[]{:S(2)}) %collective-permute-start.4) | collective-permute-done | bytes 737312 | tf_op jit(solution)/shard_map/ppermute | solution.py:327
  44.2 0.0 copy-start.2
  44.2 0.0 copy-done.1
  44.2 0.9 copy-done.2
  45.1 8.1 %zonal.1 = bf16[64,120,256]{2,1,0:T(8,128)(2,1)} custom-call(f32[1]{0:T(128)} %bitcast.sign_ref, bf16[640,768]{1,0:T(8,128)(2,1)} %constant.6.clone.even_hbm, bf16[640,768]{1,0:T(8,128)(2,1)} %constant.18.clone.odd_hbm, bf16[4,720,256]{2,1,0:T(8,128)(2,1)} %get-tuple-element.9.ka, bf16[4,720,256]{2,1,0:T(8,128)(2,1)} %copy-done.1, ...), custom_call_target="tpu_custom_call" | custom-call | flops 3019898880 | bytes 10321920 | tf_op jit(solution)/shard_map/zonal/pallas_call | solution.py:218
  53.2 62.4 %all_to_all.5.in_ref = bf16[64,120,256]{2,1,0:T(8,128)(2,1)} all-to-all(bf16[64,120,256]{2,1,0:T(8,128)(2,1)} %zonal.1), channel_id=1, replica_groups=mesh['lat'=64,'lon'=2] {'lat'}, dimensions={0} | all-to-all | bytes 7864320 | tf_op jit(solution)/shard_map/all_to_all | solution.py:331
  115.6 7.4 %gather.1 = bf16[20,384,256]{2,1,0:T(8,128)(2,1)} custom-call(bf16[64,120,256]{2,1,0:T(8,128)(2,1)} %all_to_all.5.in_ref), custom_call_target="tpu_custom_call" | custom-call | tf_op jit(solution)/shard_map/gather/pallas_call | solution.py:264
  (2 shorter events, 0.0 us)
Async XLA Ops:
  1.0 5.9 %collective-permute-start = (bf16[6,32,512]{2,1,0:T(8,128)(2,1)S(1)}, bf16[6,32,512]{2,1,0:T(8,128)(2,1)S(1)}, u32[]{:S(2)}, u32[]{:S(2)}) collective-permute-start(bf16[6,32,512]{2,1,0:T(8,128)(2,1)S(1)} %pad_maximum_fusion), channel_id=1, source_target_pairs={{0,1},{1,0},{2,3},{3,2},{4,5},{5,4},{6,7},{7,6},{8,9},{9,8},{10,11... | collective-permute-start | bytes 589832 | tf_op jit(solution)/shard_map/ppermute | solution.py:291
  6.9 4.2 %copy-start = (bf16[6,32,512]{2,1,0:T(8,128)(2,1)}, bf16[6,32,512]{2,1,0:T(8,128)(2,1)S(1)}, u32[]{:S(2)}) copy-start(bf16[6,32,512]{2,1,0:T(8,128)(2,1)S(1)} %collective-permute-done.refs_1_) | copy-start | bytes 589828
  7.0 21.2 %collective-permute-start.2 = (bf16[1,752,512]{2,1,0:T(8,128)(2,1)S(1)}, bf16[1,752,512]{2,1,0:T(8,128)(2,1)}, u32[]{:S(2)}, u32[]{:S(2)}) collective-permute-start(bf16[1,752,512]{2,1,0:T(8,128)(2,1)S(1)} %maximum_bitcast_fusion), channel_id=1, source_target_pairs={{0,2},{2,4},{4,6},{6,8},{8,10},{10,12},{12,14},{14,16},{16,18},{18... | collective-permute-start | bytes 2310152 | tf_op jit(solution)/shard_map/ppermute | solution.py:298
  11.2 20.5 %collective-permute-start.3 = (bf16[1,752,512]{2,1,0:T(8,128)(2,1)S(1)}, bf16[1,752,512]{2,1,0:T(8,128)(2,1)}, u32[]{:S(2)}, u32[]{:S(2)}) collective-permute-start(bf16[1,752,512]{2,1,0:T(8,128)(2,1)S(1)} %maximum_bitcast_fusion.1), channel_id=1, source_target_pairs={{2,0},{4,2},{6,4},{8,6},{10,8},{12,10},{14,12},{16,14},{18,16},{20... | collective-permute-start | bytes 2310152 | tf_op jit(solution)/shard_map/ppermute | solution.py:299
  27.8 14.3 %collective-permute-start.1 = (bf16[4,720,256]{2,1,0:T(8,128)(2,1)}, bf16[4,720,256]{2,1,0:T(8,128)(2,1)S(1)}, u32[]{:S(2)}, u32[]{:S(2)}) collective-permute-start(bf16[4,720,256]{2,1,0:T(8,128)(2,1)} %get-tuple-element.10), channel_id=1, source_target_pairs={{0,1},{1,0},{2,3},{3,2},{4,5},{5,4},{6,7},{7,6},{8,9},{9,8},{10,11... | collective-permute-start | bytes 4423688 | tf_op jit(solution)/shard_map/ppermute | solution.py:322
  40.9 3.3 %collective-permute-start.4 = (bf16[2,720,256]{2,1,0:T(8,128)(2,1)}, bf16[2,720,256]{2,1,0:T(8,128)(2,1)S(1)}, u32[]{:S(2)}, u32[]{:S(2)}) collective-permute-start(bf16[2,720,256]{2,1,0:T(8,128)(2,1)} %get-tuple-element.12), channel_id=1, source_target_pairs={{0,1},{1,0},{2,3},{3,2},{4,5},{5,4},{6,7},{7,6},{8,9},{9,8},{10,11... | collective-permute-start | bytes 2211848 | tf_op jit(solution)/shard_map/ppermute | solution.py:327
  42.1 2.1 %copy-start.1 = (bf16[4,720,256]{2,1,0:T(8,128)(2,1)}, bf16[4,720,256]{2,1,0:T(8,128)(2,1)S(1)}, u32[]{:S(2)}) copy-start(bf16[4,720,256]{2,1,0:T(8,128)(2,1)S(1)} %collective-permute-done.1.ra) | copy-start | bytes 4423684
  44.2 0.9 copy-start.2

commit v2 on v0

v2 whole, which is shorter than its diff:
```python
import functools

import jax
import jax.numpy as jnp
import ml_dtypes
import numpy as np
from jax import lax
from jax.experimental import pallas as pl
from jax.experimental.pallas import tpu as pltpu
from jax.sharding import PartitionSpec as P

MMAX = 640
K = 4
RLAT = 1
HMAX = 12
EDGE = 16
COLS = 48
SPAN = COLS + 2 * EDGE
DEPTH = 256
PITCH = 49
VMEM = 62 * 1024 * 1024


def exact_gelu(x):
    return 0.5 * x * (1.0 + lax.erf(x * 0.7071067811865476))


def row_kernel(joins, at, outer, lat, table_ref, own_ref, mix_hbm, even_hbm, odd_hbm, *refs):
    n_in = 2 + 2 * outer + joins
    ins, out_hbm, scratch = refs[:n_in], refs[n_in], refs[n_in + 1 :]
    ext, agg, band, added, taken, left, out, mix_ref, even_ref, odd_ref = scratch[:10]
    row_sems, own_sems, out_sems = scratch[10:]
    own = own_ref[0]
    support = table_ref.shape[1] // (K + 1)
    half_lon = ins[0].shape[1]
    total_lon = 2 * half_lon
    channels = ext.shape[2]
    rows = ext.shape[0] - 2
    groups = out.shape[0]

    def columns(side):
        return pl.ds(pl.multiple_of(EDGE + side * half_lon, 16), half_lon)

    def sides(n, mine, other, at_row):
        return (
            pltpu.make_async_copy(mine, ext.at[at_row, columns(own)], row_sems.at[n, 0]),
            pltpu.make_async_copy(other, ext.at[at_row, columns(1 - own)], row_sems.at[n, 1]),
        )

    field, swapped = ins[0], ins[1]
    if outer:
        copies = [
            sides(k, field.at[4 * own + k], swapped.at[4 * own + k], 1 - own + k) for k in (0, 1)
        ]
        copies.append(sides(2, ins[2].at[0], ins[3].at[0], 2 * own))
    else:
        copies = [sides(k, field.at[2 * own + k], swapped.at[2 * own + k], k) for k in range(rows + 2)]
    mix_copy = pltpu.make_async_copy(mix_hbm, mix_ref, own_sems.at[0])
    table_copies = (
        pltpu.make_async_copy(even_hbm, even_ref, own_sems.at[1]),
        pltpu.make_async_copy(odd_hbm, odd_ref, own_sems.at[2]),
    )
    for pair in copies[:3]:
        for copy in pair:
            copy.start()

    pad = added.shape[0] - half_lon
    added[pl.ds(half_lon, pad), :] = jnp.zeros((pad, channels), added.dtype)
    taken[pl.ds(half_lon, pad), :] = jnp.zeros((pad, channels), added.dtype)
    lanes = lax.broadcasted_iota(jnp.int32, (8, DEPTH), 1).astype(jnp.float32)

    sends = []

    def send(side, start, size, n):
        copy = pltpu.make_async_copy(
            out.at[:, side, pl.ds(start, size)],
            out_hbm.at[:, side, pl.ds(at + start, size)],
            out_sems.at[n, side],
        )
        copy.start()
        sends.append(copy)

    for step in range(rows):
        first = 0 if step == 0 else step + 2
        for pair in copies[first : step + 3]:
            for copy in pair:
                copy.wait()
        for e in range(first, step + 3):
            ext[e, pl.ds(0, EDGE), :] = ext[e, pl.ds(total_lon, EDGE), :]
            ext[e, pl.ds(EDGE + total_lon, EDGE), :] = ext[e, pl.ds(EDGE, EDGE), :]
        if step == 0:
            mix_copy.start()
            for pair in (*copies[3:], table_copies):
                for copy in pair:
                    copy.start()

        here = lat[0] + lat[1] * own + step
        filters = [jnp.zeros((8, DEPTH), jnp.float32) for _ in range(K)]
        for s in range(support):
            hit = lanes == table_ref[here, s]
            for k in range(K):
                filters[k] = filters[k] + jnp.where(hit, table_ref[here, support + s * K + k], 0.0)
        for k in range(K):
            for q in range(0, COLS, 16):
                pair = [
                    pltpu.roll(filters[k], q + e, 1, stride=1, stride_axis=0) for e in (0, 8)
                ]
                band[pl.ds(k * COLS + q, 16), :] = jnp.concatenate(pair, axis=0).astype(band.dtype)

        for start in range(0, total_lon, COLS):
            window = jnp.concatenate(
                [ext[step + r, pl.ds(start, SPAN), :] for r in range(3)]
                + [ext[step, pl.ds(start, DEPTH - 3 * SPAN), :]],
                axis=0,
            )
            got = jnp.dot(band[...], window, preferred_element_type=jnp.float32).astype(agg.dtype)
            for k in range(K):
                agg[pl.ds(start, COLS), pl.ds(k * channels, channels)] = got[k * COLS : (k + 1) * COLS]

        if step == 0:
            mix_copy.wait()
        width = channels // 2
        for n in range(0, channels, width):
            at_n = pl.ds(n, width)
            near, far = (
                exact_gelu(
                    jnp.dot(
                        agg[pl.ds(j, half_lon), :], mix_ref[:, at_n], preferred_element_type=jnp.float32
                    )
                )
                for j in (0, half_lon)
            )
            added[pl.ds(0, half_lon), at_n] = (near + far).astype(added.dtype)
            taken[pl.ds(0, half_lon), at_n] = (near - far).astype(taken.dtype)

        if step == 0:
            for copy in table_copies:
                copy.wait()
        for side in (0, 1):
            at_n = pl.ds(side * width, width)
            even = jnp.dot(even_ref[...], added[:, at_n], preferred_element_type=jnp.float32)
            odd = jnp.dot(odd_ref[...], taken[:, at_n], preferred_element_type=jnp.float32)
            main = jnp.concatenate(
                [got[: groups * 8].reshape(groups, 8, width) for got in (even, odd)], axis=1
            ).astype(out.dtype)
            for h in (0, 1):
                c = 2 * step + h
                out[:, side, pl.ds(16 * c, 16), :] = main[:, :, h * 128 : (h + 1) * 128]
                for parity, got in ((0, even), (1, odd)):
                    for e in (0, 1):
                        where = pl.ds(4 * c + 2 * e + parity, groups, stride=8 * rows)
                        rest = got[groups * (8 + e) : groups * (9 + e), h * 128 : (h + 1) * 128]
                        left[side, where, :] = rest

            send(side, 32 * step, 32, step)

    size = 8 * rows
    for side in (0, 1):
        rest = left[side].reshape(groups, size, 128)
        out[:, side, pl.ds(32 * rows, size), :] = rest.astype(out.dtype)
        send(side, 32 * rows, size, rows)
    for copy in sends:
        copy.wait()


def circle_rows(rows, at, lat, table, own, mix, even, odd, arrays, joined=None):
    _, half_lon, channels = arrays[0].shape
    groups = MMAX // 10
    smem = pl.BlockSpec(memory_space=pltpu.SMEM)
    hbm = pl.BlockSpec(memory_space=pl.ANY)
    given = list(arrays) + ([] if joined is None else [joined])
    wire = jax.ShapeDtypeStruct((groups, 2, 120, 128), jnp.bfloat16)
    return pl.pallas_call(
        functools.partial(row_kernel, int(joined is not None), at, int(len(arrays) > 2), lat),
        in_specs=[smem, smem] + [hbm] * (3 + len(given)),
        out_specs=hbm,
        out_shape=wire,
        input_output_aliases={} if joined is None else {4 + len(given): 0},
        scratch_shapes=[
            pltpu.VMEM((rows + 2, 2 * half_lon + 2 * EDGE, channels), jnp.bfloat16),
            pltpu.VMEM((2 * half_lon, K * channels), jnp.bfloat16),
            pltpu.VMEM((K * COLS, DEPTH), jnp.bfloat16),
            pltpu.VMEM((even.shape[1], channels), jnp.bfloat16),
            pltpu.VMEM((even.shape[1], channels), jnp.bfloat16),
            pltpu.VMEM((2, groups * 8 * rows, 128), jnp.float32),
            pltpu.VMEM((groups, 2, 40 * rows, 128), jnp.bfloat16),
            pltpu.VMEM(mix.shape, jnp.bfloat16),
            pltpu.VMEM(even.shape, jnp.bfloat16),
            pltpu.VMEM(odd.shape, jnp.bfloat16),
            pltpu.SemaphoreType.DMA((rows + 2, 2)),
            pltpu.SemaphoreType.DMA((3,)),
            pltpu.SemaphoreType.DMA((rows + 1, 2)),
        ],
        compiler_params=pltpu.CompilerParams(vmem_limit_bytes=VMEM),
        cost_estimate=pl.CostEstimate(
            flops=rows * (4 * half_lon * channels * (K * channels + 1024) + 4 * MMAX * half_lon * channels),
            bytes_accessed=4 * (rows + 2) * half_lon * channels + 2 * mix.size + 4 * even.size,
            transcendentals=0,
        ),
        name="circle_rows",
    )(table, own, mix, even, odd, *given)


def twiddles(total_lon, groups):
    half = total_lon // 2
    per = MMAX // groups
    cols = np.arange(half, dtype=np.int64)
    g = np.arange(groups)
    tables = []
    for parity in (0, 1):
        pairs = [(n, q) for n in g for q in range(8)] + [(n, q) for q in (8, 9) for n in g]
        group, place = np.array(pairs).T
        place = 2 * place + parity
        part, mode = place // per, group * per + place % per
        turn = (mode[:, None] * cols) % total_lon
        angles = turn.astype(np.float32) * np.float32(2.0 * np.pi / total_lon)
        scale = np.float32(1.0) / np.sqrt(np.float32(total_lon))
        table = np.zeros((MMAX, -(-half // 256) * 256), np.float32)
        table[:, :half] = np.where(part[:, None] == 0, np.cos(angles), -np.sin(angles)) * scale
        tables.append(table.astype(ml_dtypes.bfloat16))
    return tables


def gather_kernel(in_hbm, out_hbm, held, laid_0, laid_1, out, in_sems, out_sems):
    batches, sources, _, _ = held.shape
    modes, rows = out.shape[1:3]
    per = rows // sources
    laid = (laid_0, laid_1)

    def fetch(b):
        return pltpu.make_async_copy(in_hbm.at[pl.ds(b * sources, sources)], held.at[b], in_sems.at[b])

    def place(b):
        return pltpu.make_async_copy(out.at[b], out_hbm.at[:, pl.ds(b * rows, rows)], out_sems.at[b])

    def start(b, carry):
        fetch(b).start()
        return carry

    lax.fori_loop(0, batches, start, 0)

    def one(b, carry):
        fetch(b).wait()
        for g in range(sources):
            block = held[b, g].astype(jnp.float32)
            for step in range(per):
                lat = step if g % 2 else (step + 1) % per
                for h in (0, 1):
                    c = 2 * step + h
                    main, rest = (16 * c, 64 + 4 * c) if step < 2 else (80 + 16 * h, 112 + 4 * h)
                    to = g * per + lat
                    laid[h][pl.ds(to, 8, stride=PITCH), :] = block[main : main + 8]
                    laid[h][pl.ds(8 * PITCH + to, 8, stride=PITCH), :] = block[main + 8 : main + 16]
                    laid[h][pl.ds(16 * PITCH + to, 4, stride=PITCH), :] = block[rest : rest + 4]
        for m in range(modes):
            slot = 8 * (m % 2) + m // 2 if m < 16 else m
            for h in (0, 1):
                piece = laid[h][pl.ds(slot * PITCH, rows), :]
                out[b, m, :, pl.ds(128 * h, 128)] = piece.astype(out.dtype)
        place(b).start()
        return carry

    lax.fori_loop(0, batches, one, 0)

    def end(b, carry):
        place(b).wait()
        return carry

    lax.fori_loop(0, batches, end, 0)


def gather(moved):
    total, size, width = moved.shape
    sources = 16
    batches = total // sources
    modes = size // 6
    hbm = pl.BlockSpec(memory_space=pl.ANY)
    return pl.pallas_call(
        gather_kernel,
        in_specs=[hbm],
        out_specs=hbm,
        out_shape=jax.ShapeDtypeStruct((modes, total * 3, 2 * width), moved.dtype),
        scratch_shapes=[
            pltpu.VMEM((batches, sources, size, width), moved.dtype),
            pltpu.VMEM((modes * PITCH, 128), jnp.float32),
            pltpu.VMEM((modes * PITCH, 128), jnp.float32),
            pltpu.VMEM((batches, modes, sources * 3, 2 * width), moved.dtype),
            pltpu.SemaphoreType.DMA((batches,)),
            pltpu.SemaphoreType.DMA((batches,)),
        ],
        compiler_params=pltpu.CompilerParams(vmem_limit_bytes=VMEM),
        name="gather",
    )(moved)


def body(grid_field, basis_values, support_lat, support_lon, lon_reach, mix_weights):
    lat_rows, half_lon, channels = grid_field.shape
    bands = lax.axis_size("lat")
    own = lax.axis_index("lon").astype(jnp.int32)
    both = ("lat", "lon")
    last = lat_rows - 1

    swapped = lax.ppermute(grid_field, "lon", [(0, 1), (1, 0)])
    up = range(bands - 1)
    same = [(2 * b, 2 * b + 2) for b in up] + [(2 * b + 3, 2 * b + 1) for b in up]
    cross = [(2 * b + 1, 2 * b + 2) for b in up] + [(2 * b + 2, 2 * b + 1) for b in up]
    ends = (grid_field[last:], grid_field[:1])
    beside_1 = lax.ppermute(jnp.where(own == 0, *ends), both, same)
    beside_2 = lax.ppermute(jnp.where(own == 1, *ends), both, cross)

    shift = jnp.clip(support_lon, -lon_reach[:, None], lon_reach[:, None])
    index = ((support_lat + RLAT) * SPAN + EDGE + shift).astype(jnp.float32)
    basis = basis_values.astype(jnp.float32).reshape(lat_rows, -1)
    table = jnp.concatenate([index, basis], axis=1)
    mix = mix_weights.reshape(K * channels, channels)
    even, odd = (jnp.asarray(t) for t in twiddles(2 * half_lon, bands))
    own_1 = own.reshape(1)

    inner = circle_rows(2, 0, (1, 2), table, own_1, mix, even, odd, [grid_field, swapped])
    packed = circle_rows(
        1, 80, (0, last), table, own_1, mix, even, odd,
        [grid_field, swapped, beside_1, beside_2], inner,
    )
    packed = packed.reshape(2 * bands, packed.shape[2], packed.shape[3])
    moved = lax.all_to_all(packed, both, 0, 0, tiled=True)
    return gather(moved).reshape(2, MMAX // bands, bands * lat_rows, channels // 2)


def solution(mesh):
    return jax.shard_map(
        body,
        mesh=mesh,
        in_specs=(
            P("lat", "lon", None),
            P("lat", None, None),
            P("lat", None),
            P("lat", None),
            P("lat"),
            P(),
        ),
        out_specs=P(None, "lat", None, "lon"),
        check_vma=False,
    )
```

time: 832 us -> 107 us (0.13)
  local copies, waits for them, and re-layouts: 431 us -> 0.9 us
  matrix products: 254 us -> 0 us
  Pallas kernels: 0 us -> 30.6 us
  other arithmetic: 31.4 us -> 3.54 us
  loops' own time: 23.4 us -> 0 us
  blocking collectives: 78.2 us -> 65.6 us
    gather x18 -> x0, local copies, waits for them, and re-layouts: 350 us -> none  [one_row(): picked = jnp.take(flat_window, flat_index[first:last], axis=0)]
    dot_general x20 -> x0, matrix products: 254 us -> none  [the longest x18 214 us: one_row(): jnp.einsum('sjc,sk->jkc', picked, basis_row[first:last], preferred_elemen...]
    pallas_call x0 -> x3, Pallas kernels: none -> 30.6 us  [the longest x2 27.4 us: circle_rows(): pl.pallas_call(functools.partial(row_kernel, int(joined is not None), at,...]
    dynamic_slice x18 -> x0, local copies, waits for them, and re-layouts: 26.9 us -> none  [the longest x6 19.3 us: one_row(): lax.dynamic_slice(extended, (row_index, col_start - HMAX, jnp.int32(0)),...]
    another operation x1 -> x0, loops' own time: 23.4 us -> none  [aggregate_block(): lax.map(one_row, (jnp.arange(lat_rows, dtype=jnp.int32), support_lat, lon...]
    another operation x1 -> x0, other arithmetic: 17 us -> none
    all_to_all x3 -> x0, local copies, waits for them, and re-layouts: 16.2 us -> none  [the longest x1 8.29 us: body(): lax.all_to_all(activated, 'lon', split_axis=2, concat_axis=1, tiled=True)]
    unnamed x13 -> x0, local copies, waits for them, and re-layouts: 15.1 us -> none
  transfers between devices with their start and end apart: 4 -> 3, of which waited for: 2 -> 0; matrix products, arithmetic and copies ran while one was open for 2% -> 4% of each run, Pallas kernels for 0% -> 16%
where the time goes in v2:
time: 107 us
  blocking collectives  65.6 us (61%)
  Pallas kernels  30.6 us (29%)
  starting transfers between devices  5.81 us (5%)
  other arithmetic  3.54 us (3%)
    all_to_all x1, blocking collectives, body(): moved = lax.all_to_all(packed, both, 0, 0, tiled=True)  65.6 us
    pallas_call x2, Pallas kernels, circle_rows(): pl.pallas_call(functools.partial(row_kernel, int(joined is not None), at,...  27.4 us
    pallas_call x1, Pallas kernels, gather(): pl.pallas_call(gather_kernel, in_specs=[hbm], out_specs=hbm, out_shape=ja...  3.22 us
    ppermute x1, starting transfers between devices, body(): beside_2 = lax.ppermute(jnp.where(own == 1, *ends), both, cross)  3.09 us
  transfers between devices with their start and end apart: 3, of which 0 were waited for; matrix products, arithmetic and copies ran while one was open for 4% of the time, Pallas kernels for 16%

profile of v2, /device:TPU:1, one launch (start us, length us, event | category | flops | bytes accessed | tf_op | source)
XLA Modules:
  0.0 106.7 jit_solution(11982221714865667891)
XLA Ops:
  0.0 1.4 %collective-permute-start = (bf16[6,720,512]{2,1,0:T(8,128)(2,1)}, bf16[6,720,512]{2,1,0:T(8,128)(2,1)}, u32[]{:S(2)}, u32[]{:S(2)}) collective-permute-start(bf16[6,720,512]{2,1,0:T(8,128)(2,1)} %refs_0_.3), channel_id=1, source_target_pairs={{0,1},{1,0},{2,3},{3,2},{4,5},{5,4},{6,7},{7,6},{8,9},{9,8},{10,11... | collective-permute-start | bytes 13271048 | tf_op jit(solution)/shard_map/ppermute | solution.py:303
  1.4 1.4 %broadcast_select_fusion = (bf16[1,720,512]{2,1,0:T(8,128)(2,1)S(1)}, bf16[1,720,512]{2,1,0:T(8,128)(2,1)S(1)}) fusion(pred[]{:T(512)S(6)} %eq.7, bf16[6,720,512]{2,1,0:T(8,128)(2,1)} %refs_0_.3, pred[]{:T(512)S(6)} %eq.6), kind=kLoop, calls=%fused_computation | loop fusion | flops 737280 | bytes 2949122 | tf_op jit(solution)/shard_map/jit(_where)/select_n | solution.py:309
  2.9 3.1 %collective-permute-start.2 = (bf16[1,720,512]{2,1,0:T(8,128)(2,1)S(1)}, bf16[1,720,512]{2,1,0:T(8,128)(2,1)}, u32[]{:S(2)}, u32[]{:S(2)}) collective-permute-start(bf16[1,720,512]{2,1,0:T(8,128)(2,1)S(1)} %get-tuple-element.5), channel_id=1, source_target_pairs={{1,2},{3,4},{5,6},{7,8},{9,10},{11,12},{13,14},{15,16},{17,18},{19... | collective-permute-start | bytes 2211848 | tf_op jit(solution)/shard_map/ppermute | solution.py:309
  6.0 1.3 %collective-permute-start.1 = (bf16[1,720,512]{2,1,0:T(8,128)(2,1)S(1)}, bf16[1,720,512]{2,1,0:T(8,128)(2,1)}, u32[]{:S(2)}, u32[]{:S(2)}) collective-permute-start(bf16[1,720,512]{2,1,0:T(8,128)(2,1)S(1)} %get-tuple-element.6), channel_id=1, source_target_pairs={{0,2},{2,4},{4,6},{6,8},{8,10},{10,12},{12,14},{14,16},{16,18},{18... | collective-permute-start | bytes 2211848 | tf_op jit(solution)/shard_map/ppermute | solution.py:308
  7.3 0.7 neg.4
  7.9 0.8 copy.11
  8.7 0.1 reshape.28
  8.8 0.8 add_convert_fusion
  9.6 0.7 pad_maximum_fusion.table_ref
  10.3 0.0 collective-permute-done.refs_1_
  10.3 16.9 %circle_rows.2.refs_4_ = bf16[64,2,120,128]{3,2,1,0:T(8,128)(2,1)} custom-call(f32[6,120]{1,0:T(8,128)} %pad_maximum_fusion.table_ref, s32[1]{0:T(128)} %bitcast.own_ref, bf16[2048,512]{1,0:T(8,128)(2,1)} %bitcast.5, bf16[640,768]{1,0:T(8,128)(2,1)} %constant.6.clone.even_hbm, bf16[640,768]{1,0:T(8,128)(2,1)} %constant.18.clone.odd_hbm, ...), custom_call_target="tpu_custom_call" | custom-call | flops 10947133440 | bytes 9961472 | tf_op jit(solution)/shard_map/circle_rows/pallas_call | solution.py:173
  27.2 0.0 collective-permute-done.2.refs_3_
  27.2 0.0 collective-permute-done.1.refs_2_
  27.2 10.5 %circle_rows.3 = bf16[64,2,120,128]{3,2,1,0:T(8,128)(2,1)} custom-call(f32[6,120]{1,0:T(8,128)} %pad_maximum_fusion.table_ref, s32[1]{0:T(128)} %bitcast.own_ref, bf16[2048,512]{1,0:T(8,128)(2,1)} %bitcast.6, bf16[640,768]{1,0:T(8,128)(2,1)} %constant.6.clone.even_hbm, bf16[640,768]{1,0:T(8,128)(2,1)} %constant.18.clone.odd_hbm, ...), custom_call_target="tpu_custom_call", output_to_operand_aliasing={{}: (9, {})} | custom-call | flops 5473566720 | bytes 8486912 | tf_op jit(solution)/shard_map/circle_rows/pallas_call | solution.py:173
  37.7 65.6 %all_to_all.5.in_hbm = bf16[128,120,128]{2,1,0:T(8,128)(2,1)} all-to-all(bf16[128,120,128]{2,1,0:T(8,128)(2,1)} %bitcast.4), channel_id=1, replica_groups=mesh['lat'=64,'lon'=2] {'lat','lon'}, dimensions={0} | all-to-all | bytes 7864320 | tf_op jit(solution)/shard_map/all_to_all | solution.py:325
  103.3 3.2 %gather.1 = bf16[20,384,256]{2,1,0:T(8,128)(2,1)} custom-call(bf16[128,120,128]{2,1,0:T(8,128)(2,1)} %all_to_all.5.in_hbm), custom_call_target="tpu_custom_call" | custom-call | tf_op jit(solution)/shard_map/gather/pallas_call | solution.py:278
Async XLA Ops:
  0.0 10.3 %collective-permute-start = (bf16[6,720,512]{2,1,0:T(8,128)(2,1)}, bf16[6,720,512]{2,1,0:T(8,128)(2,1)}, u32[]{:S(2)}, u32[]{:S(2)}) collective-permute-start(bf16[6,720,512]{2,1,0:T(8,128)(2,1)} %refs_0_.3), channel_id=1, source_target_pairs={{0,1},{1,0},{2,3},{3,2},{4,5},{5,4},{6,7},{7,6},{8,9},{9,8},{10,11... | collective-permute-start | bytes 13271048 | tf_op jit(solution)/shard_map/ppermute | solution.py:303
  2.9 24.3 %collective-permute-start.2 = (bf16[1,720,512]{2,1,0:T(8,128)(2,1)S(1)}, bf16[1,720,512]{2,1,0:T(8,128)(2,1)}, u32[]{:S(2)}, u32[]{:S(2)}) collective-permute-start(bf16[1,720,512]{2,1,0:T(8,128)(2,1)S(1)} %get-tuple-element.5), channel_id=1, source_target_pairs={{1,2},{3,4},{5,6},{7,8},{9,10},{11,12},{13,14},{15,16},{17,18},{19... | collective-permute-start | bytes 2211848 | tf_op jit(solution)/shard_map/ppermute | solution.py:309
  6.0 21.3 %collective-permute-start.1 = (bf16[1,720,512]{2,1,0:T(8,128)(2,1)S(1)}, bf16[1,720,512]{2,1,0:T(8,128)(2,1)}, u32[]{:S(2)}, u32[]{:S(2)}) collective-permute-start(bf16[1,720,512]{2,1,0:T(8,128)(2,1)S(1)} %get-tuple-element.6), channel_id=1, source_target_pairs={{0,2},{2,4},{4,6},{6,8},{8,10},{10,12},{12,14},{14,16},{16,18},{18... | collective-permute-start | bytes 2211848 | tf_op jit(solution)/shard_map/ppermute | solution.py:308

commit v3 on v2

v3 whole, which is shorter than its diff:
```python
import functools

import jax
import jax.numpy as jnp
import ml_dtypes
import numpy as np
from jax import lax
from jax.experimental import pallas as pl
from jax.experimental.pallas import tpu as pltpu
from jax.sharding import PartitionSpec as P

MMAX = 640
K = 4
RLAT = 1
HMAX = 12
EDGE = 16
COLS = 48
SPAN = COLS + 2 * EDGE
DEPTH = 256
PITCH = 49
VMEM = 62 * 1024 * 1024


def exact_gelu(x):
    return 0.5 * x * (1.0 + lax.erf(x * 0.7071067811865476))


def row_kernel(outer, lat_ref, lon_ref, reach_ref, own_ref, basis_ref, *refs):
    mix_hbm, even_hbm, odd_hbm = refs[:3]
    n_in = 3 + 2 + 2 * outer
    ins, out_hbm, scratch = refs[3:n_in], refs[n_in], refs[n_in + 1 :]
    ext, agg, band, first, added, taken, left, out, mix_ref, even_ref, odd_ref = scratch[:11]
    row_sems, own_sems, out_sems = scratch[11:]
    own = own_ref[0]
    support = lat_ref.shape[1]
    half_lon = ins[0].shape[1]
    total_lon = 2 * half_lon
    channels = ext.shape[2]
    rows = ext.shape[0] - 2
    groups = out.shape[0]

    near_pieces = ((0, 0, half_lon), (1, 0, EDGE), (1, half_lon - EDGE, EDGE))
    pieces = (*near_pieces, (1, EDGE, half_lon - 2 * EDGE))

    def copy_of(n, p, core):
        side, begin, size = pieces[p]
        (ref, row), at_row = sources[n][side != core], sources[n][2]
        to = ext.at[at_row, pl.ds(EDGE + side * half_lon + begin, size)]
        return pltpu.make_async_copy(ref.at[row, pl.ds(begin, size)], to, row_sems.at[n, p])

    def start(n, p):
        for core in (0, 1):
            @pl.when(own == core)
            def _(core=core):
                copy_of(n, p, core).start()

    def wait(n, p):
        copy_of(n, p, 0).wait()

    field, swapped = ins[0], ins[1]
    if outer:
        sources = [((field, 3 * own + n), (swapped, 3 * own + n), 1 - own + n) for n in range(3)]
        sources.append(((ins[2], 0), (ins[3], 0), 3 * own))
        bases = [1 - own + step * (2 * own - 1) for step in range(rows)]
        lats = [4 * own + base for base in bases]
    else:
        sources = [((field, 1 + own + n), (swapped, 1 + own + n), n) for n in range(3)]
        bases, lats = [0], [2 + own]
    mix_copy = pltpu.make_async_copy(mix_hbm, mix_ref, own_sems.at[0])
    table_copies = (
        pltpu.make_async_copy(even_hbm, even_ref, own_sems.at[1]),
        pltpu.make_async_copy(odd_hbm, odd_ref, own_sems.at[2]),
    )
    for n in range(3):
        for p in range(3):
            start(n, p)
    mix_copy.start()
    for n in range(3):
        start(n, 3)
    for copy in table_copies:
        copy.start()
    for n in range(3, rows + 2):
        for p in range(4):
            start(n, p)

    pad = added.shape[0] - half_lon
    added[pl.ds(half_lon, pad), :] = jnp.zeros((pad, channels), added.dtype)
    taken[pl.ds(half_lon, pad), :] = jnp.zeros((pad, channels), added.dtype)
    sends = []

    def send(side, begin, size, n):
        copy = pltpu.make_async_copy(
            out.at[:, side, pl.ds(begin, size)],
            out_hbm.at[:, side, pl.ds(begin, size)],
            out_sems.at[n, side],
        )
        copy.start()
        sends.append(copy)

    lanes = lax.broadcasted_iota(jnp.int32, (support, DEPTH), 1)
    points = lax.broadcasted_iota(jnp.int32, (support, DEPTH), 0)
    width = channels // 2
    rest_size = 8 * rows
    for step in range(rows):
        here, base = lats[step], bases[step]
        reach = reach_ref[here]
        index = jnp.zeros((support, DEPTH), jnp.int32)
        for s in range(support):
            shift = jnp.minimum(jnp.maximum(lon_ref[here, s], -reach), reach)
            lane = (lat_ref[here, s] + RLAT) * SPAN + EDGE + shift
            index = jnp.where(points == s, lane, index)
        hits = jnp.where(lanes == index, 1.0, 0.0).astype(jnp.bfloat16)
        filters = jnp.dot(basis_ref[here], hits, preferred_element_type=jnp.float32)
        for k in range(K):
            same = jnp.broadcast_to(filters[k : k + 1], (8, DEPTH))
            for q in range(0, COLS, 16):
                pair = [pltpu.roll(same, q + e, 1, stride=1, stride_axis=0) for e in (0, 8)]
                band[pl.ds(k * COLS + q, 16), :] = jnp.concatenate(pair, axis=0).astype(band.dtype)

        fresh = range(0, 3) if step == 0 else range(step + 2, step + 3)
        for half in (0, 1):
            for n in fresh:
                for p in (range(3) if half == 0 else (3,)):
                    wait(n, p)
            if half == 0:
                for e in (sources[n][2] for n in fresh):
                    ext[e, pl.ds(0, EDGE), :] = ext[e, pl.ds(total_lon, EDGE), :]
                    ext[e, pl.ds(EDGE + total_lon, EDGE), :] = ext[e, pl.ds(EDGE, EDGE), :]
            for begin in range(half * half_lon, (half + 1) * half_lon, COLS):
                window = jnp.concatenate(
                    [ext[base + r, pl.ds(begin, SPAN), :] for r in range(3)]
                    + [ext[base, pl.ds(begin, DEPTH - 3 * SPAN), :]],
                    axis=0,
                )
                got = jnp.dot(band[...], window, preferred_element_type=jnp.float32).astype(agg.dtype)
                for k in range(K):
                    to = pl.ds(begin - half * half_lon, COLS), pl.ds(k * channels, channels)
                    agg[half, *to] = got[k * COLS : (k + 1) * COLS]
            if step == 0 and half == 0:
                mix_copy.wait()
            for n in range(0, channels, width):
                at_n = pl.ds(n, width)
                active = exact_gelu(
                    jnp.dot(agg[half], mix_ref[:, at_n], preferred_element_type=jnp.float32)
                )
                if half == 0:
                    first[:, at_n] = active
                else:
                    added[pl.ds(0, half_lon), at_n] = (first[:, at_n] + active).astype(added.dtype)
                    taken[pl.ds(0, half_lon), at_n] = (first[:, at_n] - active).astype(taken.dtype)

        if step == 0:
            for copy in table_copies:
                copy.wait()
        for side in (0, 1):
            at_n = pl.ds(side * width, width)
            even = jnp.dot(even_ref[...], added[:, at_n], preferred_element_type=jnp.float32)
            odd = jnp.dot(odd_ref[...], taken[:, at_n], preferred_element_type=jnp.float32)
            main = jnp.concatenate(
                [got[: groups * 8].reshape(groups, 8, width) for got in (even, odd)], axis=1
            ).astype(out.dtype)
            for h in (0, 1):
                c = 2 * step + h
                out[:, side, pl.ds(16 * c, 16), :] = main[:, :, h * 128 : (h + 1) * 128]
                for parity, got in ((0, even), (1, odd)):
                    for e in (0, 1):
                        where = pl.ds(4 * c + 2 * e + parity, groups, stride=rest_size)
                        rest = got[groups * (8 + e) : groups * (9 + e), h * 128 : (h + 1) * 128]
                        left[side, where, :] = rest
            send(side, 32 * step, 32, step)
            if step == rows - 1:
                rest = left[side].reshape(groups, rest_size, 128)
                out[:, side, pl.ds(32 * rows, rest_size), :] = rest.astype(out.dtype)
                send(side, 32 * rows, rest_size, rows)
    for copy in sends:
        copy.wait()


def circle_rows(rows, support, own, basis, mix, even, odd, arrays):
    _, half_lon, channels = arrays[0].shape
    groups = MMAX // 10
    smem = pl.BlockSpec(memory_space=pltpu.SMEM)
    hbm = pl.BlockSpec(memory_space=pl.ANY)
    wire = jax.ShapeDtypeStruct((groups, 2, 40 * rows, 128), jnp.bfloat16)
    return pl.pallas_call(
        functools.partial(row_kernel, int(len(arrays) > 2)),
        in_specs=[smem] * 4 + [pl.BlockSpec(memory_space=pltpu.VMEM)] + [hbm] * (3 + len(arrays)),
        out_specs=hbm,
        out_shape=wire,
        scratch_shapes=[
            pltpu.VMEM((rows + 2, 2 * half_lon + 2 * EDGE, channels), jnp.bfloat16),
            pltpu.VMEM((2, half_lon, K * channels), jnp.bfloat16),
            pltpu.VMEM((K * COLS, DEPTH), jnp.bfloat16),
            pltpu.VMEM((half_lon, channels), jnp.float32),
            pltpu.VMEM((even.shape[1], channels), jnp.bfloat16),
            pltpu.VMEM((even.shape[1], channels), jnp.bfloat16),
            pltpu.VMEM((2, groups * 8 * rows, 128), jnp.float32),
            pltpu.VMEM((groups, 2, 40 * rows, 128), jnp.bfloat16),
            pltpu.VMEM(mix.shape, jnp.bfloat16),
            pltpu.VMEM(even.shape, jnp.bfloat16),
            pltpu.VMEM(odd.shape, jnp.bfloat16),
            pltpu.SemaphoreType.DMA((rows + 2, 4)),
            pltpu.SemaphoreType.DMA((3,)),
            pltpu.SemaphoreType.DMA((rows + 1, 2)),
        ],
        compiler_params=pltpu.CompilerParams(vmem_limit_bytes=VMEM),
        cost_estimate=pl.CostEstimate(
            flops=rows * (4 * half_lon * channels * (K * channels + 1024) + 4 * MMAX * half_lon * channels),
            bytes_accessed=4 * (rows + 2) * half_lon * channels + 2 * mix.size + 4 * even.size,
            transcendentals=0,
        ),
        name="circle_rows",
    )(*support, own, basis, mix, even, odd, *arrays)


def twiddles(total_lon, groups):
    half = total_lon // 2
    per = MMAX // groups
    cols = np.arange(half, dtype=np.int64)
    g = np.arange(groups)
    tables = []
    for parity in (0, 1):
        pairs = [(n, q) for n in g for q in range(8)] + [(n, q) for q in (8, 9) for n in g]
        group, place = np.array(pairs).T
        place = 2 * place + parity
        part, mode = place // per, group * per + place % per
        turn = (mode[:, None] * cols) % total_lon
        angles = turn.astype(np.float32) * np.float32(2.0 * np.pi / total_lon)
        scale = np.float32(1.0) / np.sqrt(np.float32(total_lon))
        table = np.zeros((MMAX, -(-half // 256) * 256), np.float32)
        table[:, :half] = np.where(part[:, None] == 0, np.cos(angles), -np.sin(angles)) * scale
        tables.append(table.astype(ml_dtypes.bfloat16))
    return tables


def gather_kernel(in_1, in_2, out_hbm, held_1, held_2, laid_0, laid_1, out, in_sems, out_sems):
    batches, sources, _, _ = held_1.shape
    modes, rows = out.shape[1:3]
    per = rows // sources
    laid = (laid_0, laid_1)

    def fetch(b, n):
        ref, held = ((in_1, held_1), (in_2, held_2))[n]
        return pltpu.make_async_copy(ref.at[pl.ds(b * sources, sources)], held.at[b], in_sems.at[b, n])

    def place(b):
        return pltpu.make_async_copy(out.at[b], out_hbm.at[:, pl.ds(b * rows, rows)], out_sems.at[b])

    def start(b, carry):
        for n in (0, 1):
            fetch(b, n).start()
        return carry

    lax.fori_loop(0, batches, start, 0)

    def one(b, carry):
        for n in (0, 1):
            fetch(b, n).wait()
        for g in range(sources):
            blocks = [held[b, g].astype(jnp.float32) for held in (held_1, held_2)]
            for step in range(per):
                lat = step if g % 2 else per - 1 - step
                for h in (0, 1):
                    if step == 0:
                        block, main, rest = blocks[0], 16 * h, 32 + 4 * h
                    else:
                        c = 2 * (step - 1) + h
                        block, main, rest = blocks[1], 16 * c, 64 + 4 * c
                    to = g * per + lat
                    laid[h][pl.ds(to, 8, stride=PITCH), :] = block[main : main + 8]
                    laid[h][pl.ds(8 * PITCH + to, 8, stride=PITCH), :] = block[main + 8 : main + 16]
                    laid[h][pl.ds(16 * PITCH + to, 4, stride=PITCH), :] = block[rest : rest + 4]
        for m in range(modes):
            slot = 8 * (m % 2) + m // 2 if m < 16 else m
            for h in (0, 1):
                piece = laid[h][pl.ds(slot * PITCH, rows), :]
                out[b, m, :, pl.ds(128 * h, 128)] = piece.astype(out.dtype)
        place(b).start()
        return carry

    lax.fori_loop(0, batches, one, 0)

    def end(b, carry):
        place(b).wait()
        return carry

    lax.fori_loop(0, batches, end, 0)


def gather(moved_1, moved_2):
    total, size, width = moved_1.shape
    sources = 16
    batches = total // sources
    modes = size // 2
    hbm = pl.BlockSpec(memory_space=pl.ANY)
    return pl.pallas_call(
        gather_kernel,
        in_specs=[hbm, hbm],
        out_specs=hbm,
        out_shape=jax.ShapeDtypeStruct((modes, total * 3, 2 * width), moved_1.dtype),
        scratch_shapes=[
            pltpu.VMEM((batches, sources, size, width), moved_1.dtype),
            pltpu.VMEM((batches, sources, 2 * size, width), moved_1.dtype),
            pltpu.VMEM((modes * PITCH, 128), jnp.float32),
            pltpu.VMEM((modes * PITCH, 128), jnp.float32),
            pltpu.VMEM((batches, modes, sources * 3, 2 * width), moved_1.dtype),
            pltpu.SemaphoreType.DMA((batches, 2)),
            pltpu.SemaphoreType.DMA((batches,)),
        ],
        compiler_params=pltpu.CompilerParams(vmem_limit_bytes=VMEM),
        name="gather",
    )(moved_1, moved_2)


def body(grid_field, basis_values, support_lat, support_lon, lon_reach, mix_weights):
    lat_rows, half_lon, channels = grid_field.shape
    bands = lax.axis_size("lat")
    own = lax.axis_index("lon").astype(jnp.int32)
    both = ("lat", "lon")
    last = lat_rows - 1

    swapped = lax.ppermute(grid_field, "lon", [(0, 1), (1, 0)])
    up = range(bands - 1)
    same = [(2 * b, 2 * b + 2) for b in up] + [(2 * b + 3, 2 * b + 1) for b in up]
    cross = [(2 * b + 1, 2 * b + 2) for b in up] + [(2 * b + 2, 2 * b + 1) for b in up]
    ends = (grid_field[last:], grid_field[:1])
    beside_1 = lax.ppermute(jnp.where(own == 0, *ends), both, same)
    beside_2 = lax.ppermute(jnp.where(own == 1, *ends), both, cross)

    mix = mix_weights.reshape(K * channels, channels)
    even, odd = (jnp.asarray(t) for t in twiddles(2 * half_lon, bands))
    own_1 = own.reshape(1)

    support = (support_lat, support_lon, lon_reach)
    basis = jnp.transpose(basis_values, (0, 2, 1))
    rest = (support, own_1, basis, mix, even, odd)
    two = [grid_field, swapped]
    lone = circle_rows(1, *rest, two)
    moved_1 = lax.all_to_all(lone.reshape(2 * bands, 40, 128), both, 0, 0, tiled=True)
    pair = circle_rows(2, *rest, [*two, beside_1, beside_2])
    moved_2 = lax.all_to_all(pair.reshape(2 * bands, 80, 128), both, 0, 0, tiled=True)
    return gather(moved_1, moved_2).reshape(2, MMAX // bands, bands * lat_rows, channels // 2)


def solution(mesh):
    return jax.shard_map(
        body,
        mesh=mesh,
        in_specs=(
            P("lat", "lon", None),
            P("lat", None, None),
            P("lat", None),
            P("lat", None),
            P("lat"),
            P(),
        ),
        out_specs=P(None, "lat", None, "lon"),
        check_vma=False,
    )
```

time: 107 us -> 101 us (0.944)
  blocking collectives: 65.6 us -> 41.4 us
  starting transfers between devices: 5.81 us -> 20.8 us
  waiting for transfers between devices: 0.01 us -> 5.44 us
    all_to_all x1, blocking collectives: 65.6 us -> 41.4 us  [body(): lax.all_to_all(pair.reshape(2 * bands, 80, 128), both, 0, 0, tiled=True)]
    all_to_all x0 -> x1, starting transfers between devices: none -> 15 us  [body(): lax.all_to_all(lone.reshape(2 * bands, 40, 128), both, 0, 0, tiled=True)]
    all_to_all x0 -> x1, waiting for transfers between devices: none -> 4.92 us  [body(): lax.all_to_all(lone.reshape(2 * bands, 40, 128), both, 0, 0, tiled=True)]
    select_n x1, other arithmetic: 1.44 us -> 2.54 us  [body(): beside_2 = lax.ppermute(jnp.where(own == 1, *ends), both, cross)]
  transfers between devices with their start and end apart: 3 -> 4, of which waited for: 0 -> 2; matrix products, arithmetic and copies ran while one was open for 4% -> 3% of each run, Pallas kernels for 16% -> 27%
where the time goes in v3:
time: 101 us
  blocking collectives  41.4 us (41%)
  Pallas kernels  30.7 us (30%)
  starting transfers between devices  20.8 us (21%)
  waiting for transfers between devices  5.44 us (5%)
  other arithmetic  2.54 us (3%)
    all_to_all x1, blocking collectives, body(): lax.all_to_all(pair.reshape(2 * bands, 80, 128), both, 0, 0, tiled=True)  41.4 us
    pallas_call x2, Pallas kernels, circle_rows(): pl.pallas_call(functools.partial(row_kernel, int(len(arrays) > 2)), in_sp...  27.3 us
    all_to_all x1, starting transfers between devices, body(): lax.all_to_all(lone.reshape(2 * bands, 40, 128), both, 0, 0, tiled=True)  15 us
    all_to_all x1, waiting for transfers between devices, body(): lax.all_to_all(lone.reshape(2 * bands, 40, 128), both, 0, 0, tiled=True)  4.92 us
    pallas_call x1, Pallas kernels, gather(): pl.pallas_call(gather_kernel, in_specs=[hbm, hbm], out_specs=hbm, out_sha...  3.34 us
    ppermute x1, starting transfers between devices, body(): beside_2 = lax.ppermute(jnp.where(own == 1, *ends), both, cross)  3.08 us
    select_n x1, other arithmetic, body(): beside_2 = lax.ppermute(jnp.where(own == 1, *ends), both, cross)  2.54 us
  transfers between devices with their start and end apart: 4, of which 2 were waited for; matrix products, arithmetic and copies ran while one was open for 3% of the time, Pallas kernels for 27%

profile of v3, /device:TPU:1, one launch (start us, length us, event | category | flops | bytes accessed | tf_op | source)
XLA Modules:
  0.0 101.0 jit_solution(4245895070932672580)
XLA Ops:
  0.0 1.4 %collective-permute-start = (bf16[6,720,512]{2,1,0:T(8,128)(2,1)}, bf16[6,720,512]{2,1,0:T(8,128)(2,1)}, u32[]{:S(2)}, u32[]{:S(2)}) collective-permute-start(bf16[6,720,512]{2,1,0:T(8,128)(2,1)} %refs_3_.3), channel_id=1, source_target_pairs={{0,1},{1,0},{2,3},{3,2},{4,5},{5,4},{6,7},{7,6},{8,9},{9,8},{10,11... | collective-permute-start | bytes 13271048 | tf_op jit(solution)/shard_map/ppermute | solution.py:322
  1.4 2.5 %broadcast_select_fusion = (bf16[1,720,512]{2,1,0:T(8,128)(2,1)}, bf16[1,720,512]{2,1,0:T(8,128)(2,1)}) fusion(pred[]{:T(512)S(6)} %eq.7, bf16[6,720,512]{2,1,0:T(8,128)(2,1)} %refs_3_.3, pred[]{:T(512)S(6)} %eq.6), kind=kLoop, calls=%fused_computation | loop fusion | flops 737280 | bytes 2949122 | tf_op jit(solution)/shard_map/jit(_where)/select_n | solution.py:328
  4.0 3.1 %collective-permute-start.2 = (bf16[1,720,512]{2,1,0:T(8,128)(2,1)}, bf16[1,720,512]{2,1,0:T(8,128)(2,1)}, u32[]{:S(2)}, u32[]{:S(2)}) collective-permute-start(bf16[1,720,512]{2,1,0:T(8,128)(2,1)} %get-tuple-element.5), channel_id=1, source_target_pairs={{1,2},{3,4},{5,6},{7,8},{9,10},{11,12},{13,14},{15,16},{17,18},{19... | collective-permute-start | bytes 2211848 | tf_op jit(solution)/shard_map/ppermute | solution.py:328
  7.1 1.3 %collective-permute-start.1 = (bf16[1,720,512]{2,1,0:T(8,128)(2,1)}, bf16[1,720,512]{2,1,0:T(8,128)(2,1)}, u32[]{:S(2)}, u32[]{:S(2)}) collective-permute-start(bf16[1,720,512]{2,1,0:T(8,128)(2,1)} %get-tuple-element.6), channel_id=1, source_target_pairs={{0,2},{2,4},{4,6},{6,8},{8,10},{10,12},{12,14},{14,16},{16,18},{18... | collective-permute-start | bytes 2211848 | tf_op jit(solution)/shard_map/ppermute | solution.py:327
  8.4 0.5 collective-permute-done.refs_4_
  8.9 10.1 %circle_rows.2 = bf16[64,2,40,128]{3,2,1,0:T(8,128)(2,1)} custom-call(s32[6,24]{1,0:T(8,128)} %lat_ref.3, s32[6,24]{1,0:T(8,128)} %lon_ref.3, s32[6]{0:T(128)} %reach_ref.3, s32[1]{0:T(128)} %bitcast.own_ref, bf16[6,4,24]{2,1,0:T(4,128)(2,1)} %bitcast.10, bf16[2048,512]{1,0:T(8,128)(2,1)} %bitcast.8, bf16[640,768]{1,0:T(8,128)(2,1)} %constant.12.clone.refs_1_, ...), custom_call_target="tpu_custom_call" | custom-call | flops 5473566720 | bytes 8486912 | tf_op jit(solution)/shard_map/circle_rows/pallas_call | solution.py:185
  19.0 15.0 %all-to-all-start = ((bf16[128,40,128]{2,1,0:T(8,128)(2,1)}), bf16[128,40,128]{2,1,0:T(8,128)(2,1)S(1)}, u32[]{:S(2)}, u32[]{:S(2)}) async-start(bf16[128,40,128]{2,1,0:T(8,128)(2,1)} %bitcast.7), calls=%async_computation | async-start | bytes 2621440 | tf_op jit(solution)/shard_map/all_to_all | solution.py:339
  34.0 0.0 collective-permute-done.2.refs_6_
  34.0 0.0 collective-permute-done.1.refs_5_
  34.0 17.2 %circle_rows.3 = bf16[64,2,80,128]{3,2,1,0:T(8,128)(2,1)} custom-call(s32[6,24]{1,0:T(8,128)} %lat_ref.3, s32[6,24]{1,0:T(8,128)} %lon_ref.3, s32[6]{0:T(128)} %reach_ref.3, s32[1]{0:T(128)} %bitcast.own_ref, bf16[6,4,24]{2,1,0:T(4,128)(2,1)} %bitcast.11, bf16[2048,512]{1,0:T(8,128)(2,1)} %bitcast.9, bf16[640,768]{1,0:T(8,128)(2,1)} %constant.12.clone.refs_1_, ...), custom_call_target="tpu_custom_call" | custom-call | flops 10947133440 | bytes 9961472 | tf_op jit(solution)/shard_map/circle_rows/pallas_call | solution.py:185
  51.2 4.9 %all-to-all-done.in_1 = bf16[128,40,128]{2,1,0:T(8,128)(2,1)S(1)} async-done(((bf16[128,40,128]{2,1,0:T(8,128)(2,1)}), bf16[128,40,128]{2,1,0:T(8,128)(2,1)S(1)}, u32[]{:S(2)}, u32[]{:S(2)}) %all-to-all-start) | async-done | bytes 1310752 | tf_op jit(solution)/shard_map/all_to_all | solution.py:339
  56.1 0.0 copy-start
  56.1 41.4 %all_to_all.10.in_2 = bf16[128,80,128]{2,1,0:T(8,128)(2,1)} all-to-all(bf16[128,80,128]{2,1,0:T(8,128)(2,1)} %bitcast.6), channel_id=1, replica_groups=mesh['lat'=64,'lon'=2] {'lat','lon'}, dimensions={0} | all-to-all | bytes 5242880 | tf_op jit(solution)/shard_map/all_to_all | solution.py:341
  97.5 0.0 copy-done
  97.5 3.3 %gather.1 = bf16[20,384,256]{2,1,0:T(8,128)(2,1)} custom-call(bf16[128,40,128]{2,1,0:T(8,128)(2,1)} %copy-done, bf16[128,80,128]{2,1,0:T(8,128)(2,1)} %all_to_all.10.in_2), custom_call_target="tpu_custom_call" | custom-call | tf_op jit(solution)/shard_map/gather/pallas_call | solution.py:296
Async XLA Ops:
  0.0 8.9 %collective-permute-start = (bf16[6,720,512]{2,1,0:T(8,128)(2,1)}, bf16[6,720,512]{2,1,0:T(8,128)(2,1)}, u32[]{:S(2)}, u32[]{:S(2)}) collective-permute-start(bf16[6,720,512]{2,1,0:T(8,128)(2,1)} %refs_3_.3), channel_id=1, source_target_pairs={{0,1},{1,0},{2,3},{3,2},{4,5},{5,4},{6,7},{7,6},{8,9},{9,8},{10,11... | collective-permute-start | bytes 13271048 | tf_op jit(solution)/shard_map/ppermute | solution.py:322
  4.0 30.0 %collective-permute-start.2 = (bf16[1,720,512]{2,1,0:T(8,128)(2,1)}, bf16[1,720,512]{2,1,0:T(8,128)(2,1)}, u32[]{:S(2)}, u32[]{:S(2)}) collective-permute-start(bf16[1,720,512]{2,1,0:T(8,128)(2,1)} %get-tuple-element.5), channel_id=1, source_target_pairs={{1,2},{3,4},{5,6},{7,8},{9,10},{11,12},{13,14},{15,16},{17,18},{19... | collective-permute-start | bytes 2211848 | tf_op jit(solution)/shard_map/ppermute | solution.py:328
  7.1 26.9 %collective-permute-start.1 = (bf16[1,720,512]{2,1,0:T(8,128)(2,1)}, bf16[1,720,512]{2,1,0:T(8,128)(2,1)}, u32[]{:S(2)}, u32[]{:S(2)}) collective-permute-start(bf16[1,720,512]{2,1,0:T(8,128)(2,1)} %get-tuple-element.6), channel_id=1, source_target_pairs={{0,2},{2,4},{4,6},{6,8},{8,10},{10,12},{12,14},{14,16},{16,18},{18... | collective-permute-start | bytes 2211848 | tf_op jit(solution)/shard_map/ppermute | solution.py:327
  19.0 37.1 %all-to-all-start = ((bf16[128,40,128]{2,1,0:T(8,128)(2,1)}), bf16[128,40,128]{2,1,0:T(8,128)(2,1)S(1)}, u32[]{:S(2)}, u32[]{:S(2)}) async-start(bf16[128,40,128]{2,1,0:T(8,128)(2,1)} %bitcast.7), calls=%async_computation | async-start | bytes 2621440 | tf_op jit(solution)/shard_map/all_to_all | solution.py:339
  56.1 41.4 %copy-start = (bf16[128,40,128]{2,1,0:T(8,128)(2,1)}, bf16[128,40,128]{2,1,0:T(8,128)(2,1)S(1)}, u32[]{:S(2)}) copy-start(bf16[128,40,128]{2,1,0:T(8,128)(2,1)S(1)} %all-to-all-done.in_1) | copy-start | bytes 3932164

commit v4 on v3

--- a/solution.py
+++ b/solution.py
@@ -203,7 +203,7 @@
             pltpu.SemaphoreType.DMA((3,)),
             pltpu.SemaphoreType.DMA((rows + 1, 2)),
         ],
-        compiler_params=pltpu.CompilerParams(vmem_limit_bytes=VMEM),
+        compiler_params=pltpu.CompilerParams(vmem_limit_bytes=VMEM + (rows - 1) * 2**20),
         cost_estimate=pl.CostEstimate(
             flops=rows * (4 * half_lon * channels * (K * channels + 1024) + 4 * MMAX * half_lon * channels),
             bytes_accessed=4 * (rows + 2) * half_lon * channels + 2 * mix.size + 4 * even.size,

time: 101 us -> 100 us (0.990)
  other arithmetic: 2.54 us -> 1.44 us
    select_n x1, other arithmetic: 2.54 us -> 1.44 us  [body(): beside_2 = lax.ppermute(jnp.where(own == 1, *ends), both, cross)]
    ppermute x1, waiting for transfers between devices: 0.52 us -> 1.62 us  [body(): swapped = lax.ppermute(grid_field, 'lon', [(0, 1), (1, 0)])]
  transfers between devices with their start and end apart: 4 -> 4, of which waited for: 2 -> 2; matrix products, arithmetic and copies ran while one was open for 3% -> 1% of each run, Pallas kernels for 27% -> 27%
where the time goes in v4:
time: 100 us
  blocking collectives  41.4 us (41%)
  Pallas kernels  30.6 us (31%)
  starting transfers between devices  20.1 us (20%)
  waiting for transfers between devices  6.23 us (6%)
  other arithmetic  1.44 us (1%)
    all_to_all x1, blocking collectives, body(): lax.all_to_all(pair.reshape(2 * bands, 80, 128), both, 0, 0, tiled=True)  41.4 us
    pallas_call x2, Pallas kernels, circle_rows(): pl.pallas_call(functools.partial(row_kernel, int(len(arrays) > 2)), in_sp...  27.3 us
    all_to_all x1, starting transfers between devices, body(): lax.all_to_all(lone.reshape(2 * bands, 40, 128), both, 0, 0, tiled=True)  14.3 us
    all_to_all x1, waiting for transfers between devices, body(): lax.all_to_all(lone.reshape(2 * bands, 40, 128), both, 0, 0, tiled=True)  4.61 us
    pallas_call x1, Pallas kernels, gather(): pl.pallas_call(gather_kernel, in_specs=[hbm, hbm], out_specs=hbm, out_sha...  3.34 us
    ppermute x1, starting transfers between devices, body(): beside_2 = lax.ppermute(jnp.where(own == 1, *ends), both, cross)  3.09 us
  transfers between devices with their start and end apart: 4, of which 2 were waited for; matrix products, arithmetic and copies ran while one was open for 1% of the time, Pallas kernels for 27%

profile of v4, /device:TPU:1, one launch (start us, length us, event | category | flops | bytes accessed | tf_op | source)
XLA Modules:
  0.0 100.0 jit_solution(2940162754569683543)
XLA Ops:
  0.0 1.4 %collective-permute-start = (bf16[6,720,512]{2,1,0:T(8,128)(2,1)}, bf16[6,720,512]{2,1,0:T(8,128)(2,1)}, u32[]{:S(2)}, u32[]{:S(2)}) collective-permute-start(bf16[6,720,512]{2,1,0:T(8,128)(2,1)} %refs_3_.3), channel_id=1, source_target_pairs={{0,1},{1,0},{2,3},{3,2},{4,5},{5,4},{6,7},{7,6},{8,9},{9,8},{10,11... | collective-permute-start | bytes 13271048 | tf_op jit(solution)/shard_map/ppermute | solution.py:322
  1.4 1.4 %broadcast_select_fusion = (bf16[1,720,512]{2,1,0:T(8,128)(2,1)S(1)}, bf16[1,720,512]{2,1,0:T(8,128)(2,1)S(1)}) fusion(pred[]{:T(512)S(6)} %eq.7, bf16[6,720,512]{2,1,0:T(8,128)(2,1)} %refs_3_.3, pred[]{:T(512)S(6)} %eq.6), kind=kLoop, calls=%fused_computation | loop fusion | flops 737280 | bytes 2949122 | tf_op jit(solution)/shard_map/jit(_where)/select_n | solution.py:328
  2.9 3.1 %collective-permute-start.2 = (bf16[1,720,512]{2,1,0:T(8,128)(2,1)S(1)}, bf16[1,720,512]{2,1,0:T(8,128)(2,1)}, u32[]{:S(2)}, u32[]{:S(2)}) collective-permute-start(bf16[1,720,512]{2,1,0:T(8,128)(2,1)S(1)} %get-tuple-element.5), channel_id=1, source_target_pairs={{1,2},{3,4},{5,6},{7,8},{9,10},{11,12},{13,14},{15,16},{17,18},{19... | collective-permute-start | bytes 2211848 | tf_op jit(solution)/shard_map/ppermute | solution.py:328
  6.0 1.3 %collective-permute-start.1 = (bf16[1,720,512]{2,1,0:T(8,128)(2,1)S(1)}, bf16[1,720,512]{2,1,0:T(8,128)(2,1)}, u32[]{:S(2)}, u32[]{:S(2)}) collective-permute-start(bf16[1,720,512]{2,1,0:T(8,128)(2,1)S(1)} %get-tuple-element.6), channel_id=1, source_target_pairs={{0,2},{2,4},{4,6},{6,8},{8,10},{10,12},{12,14},{14,16},{16,18},{18... | collective-permute-start | bytes 2211848 | tf_op jit(solution)/shard_map/ppermute | solution.py:327
  7.3 1.6 %collective-permute-done.refs_4_ = bf16[6,720,512]{2,1,0:T(8,128)(2,1)} collective-permute-done((bf16[6,720,512]{2,1,0:T(8,128)(2,1)}, bf16[6,720,512]{2,1,0:T(8,128)(2,1)}, u32[]{:S(2)}, u32[]{:S(2)}) %collective-permute-start) | collective-permute-done | bytes 4423712 | tf_op jit(solution)/shard_map/ppermute | solution.py:322
  8.9 10.1 %circle_rows.2 = bf16[64,2,40,128]{3,2,1,0:T(8,128)(2,1)} custom-call(s32[6,24]{1,0:T(8,128)} %lat_ref.3, s32[6,24]{1,0:T(8,128)} %lon_ref.3, s32[6]{0:T(128)} %reach_ref.3, s32[1]{0:T(128)} %bitcast.own_ref, bf16[6,4,24]{2,1,0:T(4,128)(2,1)} %bitcast.10, bf16[2048,512]{1,0:T(8,128)(2,1)} %bitcast.8, bf16[640,768]{1,0:T(8,128)(2,1)} %constant.12.clone.refs_1_, ...), custom_call_target="tpu_custom_call" | custom-call | flops 5473566720 | bytes 8486912 | tf_op jit(solution)/shard_map/circle_rows/pallas_call | solution.py:185
  19.0 14.3 %all-to-all-start = ((bf16[128,40,128]{2,1,0:T(8,128)(2,1)}), bf16[128,40,128]{2,1,0:T(8,128)(2,1)}, u32[]{:S(2)}, u32[]{:S(2)}) async-start(bf16[128,40,128]{2,1,0:T(8,128)(2,1)} %bitcast.7), calls=%async_computation | async-start | bytes 2621440 | tf_op jit(solution)/shard_map/all_to_all | solution.py:339
  33.3 0.0 collective-permute-done.2.refs_6_
  33.3 0.0 collective-permute-done.1.refs_5_
  33.3 17.2 %circle_rows.3 = bf16[64,2,80,128]{3,2,1,0:T(8,128)(2,1)} custom-call(s32[6,24]{1,0:T(8,128)} %lat_ref.3, s32[6,24]{1,0:T(8,128)} %lon_ref.3, s32[6]{0:T(128)} %reach_ref.3, s32[1]{0:T(128)} %bitcast.own_ref, bf16[6,4,24]{2,1,0:T(4,128)(2,1)} %bitcast.11, bf16[2048,512]{1,0:T(8,128)(2,1)} %bitcast.9, bf16[640,768]{1,0:T(8,128)(2,1)} %constant.12.clone.refs_1_, ...), custom_call_target="tpu_custom_call" | custom-call | flops 10947133440 | bytes 9961472 | tf_op jit(solution)/shard_map/circle_rows/pallas_call | solution.py:185
  50.5 4.6 %all-to-all-done.in_1 = bf16[128,40,128]{2,1,0:T(8,128)(2,1)} async-done(((bf16[128,40,128]{2,1,0:T(8,128)(2,1)}), bf16[128,40,128]{2,1,0:T(8,128)(2,1)}, u32[]{:S(2)}, u32[]{:S(2)}) %all-to-all-start) | async-done | bytes 1310752 | tf_op jit(solution)/shard_map/all_to_all | solution.py:339
  55.1 41.4 %all_to_all.10.in_2 = bf16[128,80,128]{2,1,0:T(8,128)(2,1)} all-to-all(bf16[128,80,128]{2,1,0:T(8,128)(2,1)} %bitcast.6), channel_id=1, replica_groups=mesh['lat'=64,'lon'=2] {'lat','lon'}, dimensions={0} | all-to-all | bytes 5242880 | tf_op jit(solution)/shard_map/all_to_all | solution.py:341
  96.5 3.3 %gather.1 = bf16[20,384,256]{2,1,0:T(8,128)(2,1)} custom-call(bf16[128,40,128]{2,1,0:T(8,128)(2,1)} %all-to-all-done.in_1, bf16[128,80,128]{2,1,0:T(8,128)(2,1)} %all_to_all.10.in_2), custom_call_target="tpu_custom_call" | custom-call | tf_op jit(solution)/shard_map/gather/pallas_call | solution.py:296
Async XLA Ops:
  0.0 8.9 %collective-permute-start = (bf16[6,720,512]{2,1,0:T(8,128)(2,1)}, bf16[6,720,512]{2,1,0:T(8,128)(2,1)}, u32[]{:S(2)}, u32[]{:S(2)}) collective-permute-start(bf16[6,720,512]{2,1,0:T(8,128)(2,1)} %refs_3_.3), channel_id=1, source_target_pairs={{0,1},{1,0},{2,3},{3,2},{4,5},{5,4},{6,7},{7,6},{8,9},{9,8},{10,11... | collective-permute-start | bytes 13271048 | tf_op jit(solution)/shard_map/ppermute | solution.py:322
  2.9 30.4 %collective-permute-start.2 = (bf16[1,720,512]{2,1,0:T(8,128)(2,1)S(1)}, bf16[1,720,512]{2,1,0:T(8,128)(2,1)}, u32[]{:S(2)}, u32[]{:S(2)}) collective-permute-start(bf16[1,720,512]{2,1,0:T(8,128)(2,1)S(1)} %get-tuple-element.5), channel_id=1, source_target_pairs={{1,2},{3,4},{5,6},{7,8},{9,10},{11,12},{13,14},{15,16},{17,18},{19... | collective-permute-start | bytes 2211848 | tf_op jit(solution)/shard_map/ppermute | solution.py:328
  6.0 27.3 %collective-permute-start.1 = (bf16[1,720,512]{2,1,0:T(8,128)(2,1)S(1)}, bf16[1,720,512]{2,1,0:T(8,128)(2,1)}, u32[]{:S(2)}, u32[]{:S(2)}) collective-permute-start(bf16[1,720,512]{2,1,0:T(8,128)(2,1)S(1)} %get-tuple-element.6), channel_id=1, source_target_pairs={{0,2},{2,4},{4,6},{6,8},{8,10},{10,12},{12,14},{14,16},{16,18},{18... | collective-permute-start | bytes 2211848 | tf_op jit(solution)/shard_map/ppermute | solution.py:327
  19.0 36.1 %all-to-all-start = ((bf16[128,40,128]{2,1,0:T(8,128)(2,1)}), bf16[128,40,128]{2,1,0:T(8,128)(2,1)}, u32[]{:S(2)}, u32[]{:S(2)}) async-start(bf16[128,40,128]{2,1,0:T(8,128)(2,1)} %bitcast.7), calls=%async_computation | async-start | bytes 2621440 | tf_op jit(solution)/shard_map/all_to_all | solution.py:339

commit v5 on v4

--- a/solution.py
+++ b/solution.py
@@ -47,12 +47,6 @@
         (ref, row), at_row = sources[n][side != core], sources[n][2]
         to = ext.at[at_row, pl.ds(EDGE + side * half_lon + begin, size)]
         return pltpu.make_async_copy(ref.at[row, pl.ds(begin, size)], to, row_sems.at[n, p])
-
-    def start(n, p):
-        for core in (0, 1):
-            @pl.when(own == core)
-            def _(core=core):
-                copy_of(n, p, core).start()
 
     def wait(n, p):
         copy_of(n, p, 0).wait()
@@ -71,17 +65,20 @@
         pltpu.make_async_copy(even_hbm, even_ref, own_sems.at[1]),
         pltpu.make_async_copy(odd_hbm, odd_ref, own_sems.at[2]),
     )
-    for n in range(3):
-        for p in range(3):
-            start(n, p)
-    mix_copy.start()
-    for n in range(3):
-        start(n, 3)
-    for copy in table_copies:
-        copy.start()
-    for n in range(3, rows + 2):
-        for p in range(4):
-            start(n, p)
+    for core in (0, 1):
+        @pl.when(own == core)
+        def _(core=core):
+            for n in range(3):
+                for p in range(3):
+                    copy_of(n, p, core).start()
+            mix_copy.start()
+            for n in range(3):
+                copy_of(n, 3, core).start()
+            for copy in table_copies:
+                copy.start()
+            for n in range(3, rows + 2):
+                for p in range(4):
+                    copy_of(n, p, core).start()
 
     pad = added.shape[0] - half_lon
     added[pl.ds(half_lon, pad), :] = jnp.zeros((pad, channels), added.dtype)

time: 100 us -> 101 us (1.010)
  transfers between devices with their start and end apart: 4 -> 4, of which waited for: 2 -> 2; matrix products, arithmetic and copies ran while one was open for 1% -> 1% of each run, Pallas kernels for 27% -> 28%
where the time goes in v5:
time: 101 us; the launch traced here: 100 us
  blocking collectives  41.5 us (41%)
  Pallas kernels  31.1 us (31%)
  starting transfers between devices  20 us (20%)
  waiting for transfers between devices  6.09 us (6%)
  other arithmetic  1.44 us (1%)
    all_to_all x1, blocking collectives, body(): lax.all_to_all(pair.reshape(2 * bands, 80, 128), both, 0, 0, tiled=True)  41.5 us
    pallas_call x2, Pallas kernels, circle_rows(): pl.pallas_call(functools.partial(row_kernel, int(len(arrays) > 2)), in_sp...  27.8 us
    all_to_all x1, starting transfers between devices, body(): lax.all_to_all(lone.reshape(2 * bands, 40, 128), both, 0, 0, tiled=True)  14.2 us
    all_to_all x1, waiting for transfers between devices, body(): lax.all_to_all(lone.reshape(2 * bands, 40, 128), both, 0, 0, tiled=True)  4.47 us
    pallas_call x1, Pallas kernels, gather(): pl.pallas_call(gather_kernel, in_specs=[hbm, hbm], out_specs=hbm, out_sha...  3.34 us
    ppermute x1, starting transfers between devices, body(): beside_2 = lax.ppermute(jnp.where(own == 1, *ends), both, cross)  3.09 us
  transfers between devices with their start and end apart: 4, of which 2 were waited for; matrix products, arithmetic and copies ran while one was open for 1% of the time, Pallas kernels for 28%

profile of v5, /device:TPU:1, one launch (start us, length us, event | category | flops | bytes accessed | tf_op | source)
XLA Modules:
  0.0 100.3 jit_solution(2361827140910249666)
XLA Ops:
  0.0 1.4 %collective-permute-start = (bf16[6,720,512]{2,1,0:T(8,128)(2,1)}, bf16[6,720,512]{2,1,0:T(8,128)(2,1)}, u32[]{:S(2)}, u32[]{:S(2)}) collective-permute-start(bf16[6,720,512]{2,1,0:T(8,128)(2,1)} %refs_3_.3), channel_id=1, source_target_pairs={{0,1},{1,0},{2,3},{3,2},{4,5},{5,4},{6,7},{7,6},{8,9},{9,8},{10,11... | collective-permute-start | bytes 13271048 | tf_op jit(solution)/shard_map/ppermute | solution.py:319
  1.4 1.4 %broadcast_select_fusion = (bf16[1,720,512]{2,1,0:T(8,128)(2,1)S(1)}, bf16[1,720,512]{2,1,0:T(8,128)(2,1)S(1)}) fusion(pred[]{:T(512)S(6)} %eq.7, bf16[6,720,512]{2,1,0:T(8,128)(2,1)} %refs_3_.3, pred[]{:T(512)S(6)} %eq.6), kind=kLoop, calls=%fused_computation | loop fusion | flops 737280 | bytes 2949122 | tf_op jit(solution)/shard_map/jit(_where)/select_n | solution.py:325
  2.9 3.1 %collective-permute-start.2 = (bf16[1,720,512]{2,1,0:T(8,128)(2,1)S(1)}, bf16[1,720,512]{2,1,0:T(8,128)(2,1)}, u32[]{:S(2)}, u32[]{:S(2)}) collective-permute-start(bf16[1,720,512]{2,1,0:T(8,128)(2,1)S(1)} %get-tuple-element.5), channel_id=1, source_target_pairs={{1,2},{3,4},{5,6},{7,8},{9,10},{11,12},{13,14},{15,16},{17,18},{19... | collective-permute-start | bytes 2211848 | tf_op jit(solution)/shard_map/ppermute | solution.py:325
  6.0 1.3 %collective-permute-start.1 = (bf16[1,720,512]{2,1,0:T(8,128)(2,1)S(1)}, bf16[1,720,512]{2,1,0:T(8,128)(2,1)}, u32[]{:S(2)}, u32[]{:S(2)}) collective-permute-start(bf16[1,720,512]{2,1,0:T(8,128)(2,1)S(1)} %get-tuple-element.6), channel_id=1, source_target_pairs={{0,2},{2,4},{4,6},{6,8},{8,10},{10,12},{12,14},{14,16},{16,18},{18... | collective-permute-start | bytes 2211848 | tf_op jit(solution)/shard_map/ppermute | solution.py:324
  7.3 1.6 %collective-permute-done.refs_4_ = bf16[6,720,512]{2,1,0:T(8,128)(2,1)} collective-permute-done((bf16[6,720,512]{2,1,0:T(8,128)(2,1)}, bf16[6,720,512]{2,1,0:T(8,128)(2,1)}, u32[]{:S(2)}, u32[]{:S(2)}) %collective-permute-start) | collective-permute-done | bytes 4423712 | tf_op jit(solution)/shard_map/ppermute | solution.py:319
  8.9 10.4 %circle_rows.2 = bf16[64,2,40,128]{3,2,1,0:T(8,128)(2,1)} custom-call(s32[6,24]{1,0:T(8,128)} %lat_ref.3, s32[6,24]{1,0:T(8,128)} %lon_ref.3, s32[6]{0:T(128)} %reach_ref.3, s32[1]{0:T(128)} %bitcast.own_ref, bf16[6,4,24]{2,1,0:T(4,128)(2,1)} %bitcast.10, bf16[2048,512]{1,0:T(8,128)(2,1)} %bitcast.8, bf16[640,768]{1,0:T(8,128)(2,1)} %constant.12.clone.refs_1_, ...), custom_call_target="tpu_custom_call" | custom-call | flops 5473566720 | bytes 8486912 | tf_op jit(solution)/shard_map/circle_rows/pallas_call | solution.py:182
  19.3 14.2 %all-to-all-start = ((bf16[128,40,128]{2,1,0:T(8,128)(2,1)}), bf16[128,40,128]{2,1,0:T(8,128)(2,1)}, u32[]{:S(2)}, u32[]{:S(2)}) async-start(bf16[128,40,128]{2,1,0:T(8,128)(2,1)} %bitcast.7), calls=%async_computation | async-start | bytes 2621440 | tf_op jit(solution)/shard_map/all_to_all | solution.py:336
  33.5 0.0 collective-permute-done.2.refs_6_
  33.5 0.0 collective-permute-done.1.refs_5_
  33.5 17.3 %circle_rows.3 = bf16[64,2,80,128]{3,2,1,0:T(8,128)(2,1)} custom-call(s32[6,24]{1,0:T(8,128)} %lat_ref.3, s32[6,24]{1,0:T(8,128)} %lon_ref.3, s32[6]{0:T(128)} %reach_ref.3, s32[1]{0:T(128)} %bitcast.own_ref, bf16[6,4,24]{2,1,0:T(4,128)(2,1)} %bitcast.11, bf16[2048,512]{1,0:T(8,128)(2,1)} %bitcast.9, bf16[640,768]{1,0:T(8,128)(2,1)} %constant.12.clone.refs_1_, ...), custom_call_target="tpu_custom_call" | custom-call | flops 10947133440 | bytes 9961472 | tf_op jit(solution)/shard_map/circle_rows/pallas_call | solution.py:182
  50.9 4.5 %all-to-all-done.in_1 = bf16[128,40,128]{2,1,0:T(8,128)(2,1)} async-done(((bf16[128,40,128]{2,1,0:T(8,128)(2,1)}), bf16[128,40,128]{2,1,0:T(8,128)(2,1)}, u32[]{:S(2)}, u32[]{:S(2)}) %all-to-all-start) | async-done | bytes 1310752 | tf_op jit(solution)/shard_map/all_to_all | solution.py:336
  55.3 41.5 %all_to_all.10.in_2 = bf16[128,80,128]{2,1,0:T(8,128)(2,1)} all-to-all(bf16[128,80,128]{2,1,0:T(8,128)(2,1)} %bitcast.6), channel_id=1, replica_groups=mesh['lat'=64,'lon'=2] {'lat','lon'}, dimensions={0} | all-to-all | bytes 5242880 | tf_op jit(solution)/shard_map/all_to_all | solution.py:338
  96.8 3.3 %gather.1 = bf16[20,384,256]{2,1,0:T(8,128)(2,1)} custom-call(bf16[128,40,128]{2,1,0:T(8,128)(2,1)} %all-to-all-done.in_1, bf16[128,80,128]{2,1,0:T(8,128)(2,1)} %all_to_all.10.in_2), custom_call_target="tpu_custom_call" | custom-call | tf_op jit(solution)/shard_map/gather/pallas_call | solution.py:293
Async XLA Ops:
  0.0 8.9 %collective-permute-start = (bf16[6,720,512]{2,1,0:T(8,128)(2,1)}, bf16[6,720,512]{2,1,0:T(8,128)(2,1)}, u32[]{:S(2)}, u32[]{:S(2)}) collective-permute-start(bf16[6,720,512]{2,1,0:T(8,128)(2,1)} %refs_3_.3), channel_id=1, source_target_pairs={{0,1},{1,0},{2,3},{3,2},{4,5},{5,4},{6,7},{7,6},{8,9},{9,8},{10,11... | collective-permute-start | bytes 13271048 | tf_op jit(solution)/shard_map/ppermute | solution.py:319
  2.9 30.6 %collective-permute-start.2 = (bf16[1,720,512]{2,1,0:T(8,128)(2,1)S(1)}, bf16[1,720,512]{2,1,0:T(8,128)(2,1)}, u32[]{:S(2)}, u32[]{:S(2)}) collective-permute-start(bf16[1,720,512]{2,1,0:T(8,128)(2,1)S(1)} %get-tuple-element.5), channel_id=1, source_target_pairs={{1,2},{3,4},{5,6},{7,8},{9,10},{11,12},{13,14},{15,16},{17,18},{19... | collective-permute-start | bytes 2211848 | tf_op jit(solution)/shard_map/ppermute | solution.py:325
  6.0 27.5 %collective-permute-start.1 = (bf16[1,720,512]{2,1,0:T(8,128)(2,1)S(1)}, bf16[1,720,512]{2,1,0:T(8,128)(2,1)}, u32[]{:S(2)}, u32[]{:S(2)}) collective-permute-start(bf16[1,720,512]{2,1,0:T(8,128)(2,1)S(1)} %get-tuple-element.6), channel_id=1, source_target_pairs={{0,2},{2,4},{4,6},{6,8},{8,10},{10,12},{12,14},{14,16},{16,18},{18... | collective-permute-start | bytes 2211848 | tf_op jit(solution)/shard_map/ppermute | solution.py:324
  19.3 36.0 %all-to-all-start = ((bf16[128,40,128]{2,1,0:T(8,128)(2,1)}), bf16[128,40,128]{2,1,0:T(8,128)(2,1)}, u32[]{:S(2)}, u32[]{:S(2)}) async-start(bf16[128,40,128]{2,1,0:T(8,128)(2,1)} %bitcast.7), calls=%async_computation | async-start | bytes 2621440 | tf_op jit(solution)/shard_map/all_to_all | solution.py:336
